TPU v7x, 128 devices: a whole 4x4x4 slice. The times are simulated.
128 devices in a mesh: feat: 16 (over z, x), dp: 8 (over y, core).
Axes of the slice: x: 4, y: 4, z: 4, core: 2. Of those that a mesh axis runs over, the one named last changes fastest.
Arguments:
- node_table: bfloat16 [768, 65536], P('feat'), may hold values from -6 to 6
- neighbor_ids: int32 [384, 26, 128], P('dp'), may hold values from 0 to 65535
- tile_counts: int32 [128], P(('dp', 'feat')), may hold values from 1 to 3, as said below
- w_self: bfloat16 [768, 1024], P('feat'), may hold values from -0.21875 to 0.21875
- w_neigh: bfloat16 [768, 1024], P('feat'), may hold values from -0.4375 to 0.4375
- bias: float32 [1024], replicated, may hold values from -1 to 1
- cotangent: bfloat16 [384, 128, 1024], P(('dp', 'feat')), may hold values from -6 to 6
Outputs:
- activations: bfloat16 [384, 128, 1024], P(('dp', 'feat'))
- grad_self: float32 [768, 1024], P('feat')
- grad_neigh: float32 [768, 1024], P('feat')
Inputs may be any that keep to these rules, and one draw needn't show every extreme that they name: `tile_counts`: some minibatch fills all 3 slots.
All inputs are finite; a program needn't handle non-finite values.
Results may differ from a plain program's by a relative error of at most 0.018.
The roundings to bfloat16 on the way count: a program that leaves them out, or rounds other values in their place, can miss the bound.
Values may be sent and summed in bfloat16 or wider, within the bound.
A program may use at most 192 MiB of HBM per device.

v0:
```python
import jax
import jax.numpy as jnp
from jax import lax
from jax.sharding import PartitionSpec as P


def local(node_table, neighbor_ids, tile_counts, w_self, w_neigh, bias, cotangent):
    block, nodes = node_table.shape
    groups, fan_one, rows = neighbor_ids.shape
    owned = cotangent.shape[0]
    gathered = jnp.take(node_table, neighbor_ids.reshape(-1), axis=1).reshape(
        block, groups, fan_one, rows
    )
    own = gathered[:, :, 0]
    summed = jnp.sum(gathered[:, :, 1:], axis=2, dtype=jnp.float32) / (fan_one - 1)
    mean = summed.astype(jnp.bfloat16)
    live = jnp.arange(owned, dtype=jnp.int32) < tile_counts[0]
    own_part = own
    mean_part = mean
    term = jnp.einsum("ftr,fh->trh", own_part, w_self, preferred_element_type=jnp.float32)
    pre = (
        lax.psum_scatter(
            term
            + jnp.einsum("ftr,fh->trh", mean_part, w_neigh, preferred_element_type=jnp.float32),
            "feat",
            scatter_dimension=0,
            tiled=True,
        )
        + bias
    )
    live_mask = live[:, None, None]
    activations = jnp.where(live_mask, jnp.maximum(pre, 0.0), 0.0).astype(jnp.bfloat16)
    delta = jnp.where(live_mask & (pre > 0), cotangent, jnp.zeros_like(cotangent))
    piece = lax.all_gather(delta, "feat", axis=0, tiled=True)
    own_part = own
    mean_part = mean
    grad_a = jnp.einsum("ftr,trh->fh", own_part, piece, preferred_element_type=jnp.float32)
    grad_b = jnp.einsum("ftr,trh->fh", mean_part, piece, preferred_element_type=jnp.float32)
    grad_self, grad_neigh = (
        lax.psum(grad_a.astype(jnp.bfloat16), "dp").astype(jnp.float32),
        lax.psum(grad_b.astype(jnp.bfloat16), "dp").astype(jnp.float32),
    )
    return (activations, grad_self, grad_neigh)


def solution(mesh):
    return jax.shard_map(
        local,
        mesh=mesh,
        in_specs=(
            P("feat", None),
            P("dp", None, None),
            P(("dp", "feat")),
            P("feat", None),
            P("feat", None),
            P(),
            P(("dp", "feat"), None, None),
        ),
        out_specs=(P(("dp", "feat"), None, None), P("feat", None), P("feat", None)),
        check_vma=False,
    )
```

profile of v0, /device:TPU:1, one launch (start us, length us, event | category | flops | bytes accessed | tf_op | source)
XLA Modules:
  0.0 981.3 jit_solution(16523307943526643220)
XLA Ops:
  7.2 0.0 copy-start
  7.2 0.0 reduce-scatter.4.cloned.1.call-start
  7.2 1.3 copy.15
  8.5 1.3 compare_and_fusion
  9.8 15.1 %copy.16 = bf16[48,65536]{0,1:T(8,128)(2,1)} copy(bf16[48,65536]{1,0:T(8,128)(2,1)} %param.7) | data formatting | bytes 12582912 | tf_op args[0]
  24.9 0.6 reshape.54
  25.6 0.7 compare_select_fusion
  26.3 0.1 broadcast_clamp_fusion
  26.4 541.5 %gather_fusion = bf16[159744,48]{1,0:T(8,128)(2,1)} fusion(bf16[48,65536]{0,1:T(8,128)(2,1)} %copy.16, s32[159744]{0:T(1024)S(1)} %broadcast_clamp_fusion), kind=kCustom, calls=%fused_computation | custom fusion | bytes 31309824 | tf_op jit(solution)/shard_map/jit(_take)/gather | solution.py:11
  567.9 36.1 %copy.18 = bf16[48,48,26,128]{3,0,1,2:T(8,128)(2,1)} copy(bf16[48,48,26,128]{0,3,2,1:T(8,128)(2,1)} %bitcast.27) | data formatting | bytes 30670848 | tf_op jit(solution)/shard_map/jit(_take)/gather | solution.py:11
  604.0 13.4 %broadcast_select_fusion = bf16[48,48,26,128]{3,0,1,2:T(8,128)(2,1)} fusion(bf16[48,48,26,128]{3,0,1,2:T(8,128)(2,1)} %copy.18, pred[48,26,128]{2,0,1:T(8,128)(4,1)S(1)} %compare_and_fusion), kind=kLoop, calls=%fused_computation.2 | loop fusion | flops 7667712 | bytes 30830592 | tf_op jit(solution)/shard_map/jit(_take)/select_n | solution.py:11
  617.4 7.4 convert_reduce_fusion
  624.9 0.0 copy-done
  624.9 0.0 copy-start.4
  624.9 11.2 %fusion.2 = f32[48,128,1024]{2,1,0:T(8,128)} fusion(bf16[48,48,26,128]{3,0,1,2:T(8,128)(2,1)} %broadcast_select_fusion, bf16[48,1024]{1,0:T(8,128)(2,1)S(1)} %copy-done), kind=kOutput, calls=%fused_computation.15 | convolution fusion | flops 603979776 | bytes 25853952 | tf_op jit(solution)/shard_map/ftr,fh->trh/dot_general | solution.py:20
  636.1 0.0 copy-done.4
  636.1 16.3 %convolution_add_fusion = f32[48,128,1024]{2,1,0:T(8,128)} fusion(f32[48,128,1024]{2,1,0:T(8,128)} %fusion.2, f32[48,48,128]{2,0,1:T(8,128)S(1)} %convert_reduce_fusion, bf16[48,1024]{1,0:T(8,128)(2,1)S(1)} %copy-done.4), kind=kOutput, calls=%fused_computation.3 | convolution fusion | flops 610861056 | bytes 51609600 | tf_op jit(solution)/shard_map/ftr,fh->trh/dot_general | solution.py:24
  652.4 0.0 copy-start.3
  652.4 0.0 copy-start.5
  652.4 0.0 reduce-scatter.4.cloned.1.call-update
  652.5 0.0 all-gather.2.cloned.1.call-start
  653.2 155.9 %reduce-scatter.4.cloned.1.call-done = f32[3,128,1024]{2,1,0:T(8,128)} async-done(((f32[48,128,1024]{2,1,0:T(8,128)}), f32[3,128,1024]{2,1,0:T(8,128)}) %reduce-scatter.4.cloned.1.call-update) | async-done | bytes 1572880
  809.1 0.0 copy-done.3
  809.1 0.0 copy-done.5
  809.1 2.7 and_select_fusion
  811.8 0.0 all-gather.2.cloned.1.call-update
  811.9 0.2 all-reduce.4.cloned.1.call-start
  812.1 89.7 %all-gather.2.cloned.1.call-done = bf16[48,128,1024]{2,1,0:T(8,128)(2,1)} async-done(((bf16[3,128,1024]{2,1,0:T(8,128)(2,1)}), bf16[48,128,1024]{2,1,0:T(8,128)(2,1)}) %all-gather.2.cloned.1.call-update) | async-done | bytes 12582928 | tf_op jit(solution)/shard_map/all_gather | solution.py:34
  901.8 0.0 copy-start.1
  901.8 7.2 fusion.1
  909.0 1.0 copy-done.1
  910.0 0.0 copy-start.2
  910.0 4.1 fusion
  914.1 0.0 all-reduce.4.cloned.1.call-update
  914.1 0.0 copy-done.2
  914.2 1.2 select_convert_fusion
  915.3 56.2 %all-reduce.4.cloned.1.call-done = (bf16[48,1024]{1,0:T(8,128)(2,1)}, bf16[48,1024]{1,0:T(8,128)(2,1)}) async-done(((bf16[48,1024]{1,0:T(8,128)(2,1)}, bf16[48,1024]{1,0:T(8,128)(2,1)}), (bf16[48,1024]{1,0:T(8,128)(2,1)}, bf16[48,1024]{1,0:T(8,128)(2,1)})) %all-reduce.4.cloned.1.call-update) | async-done | bytes 196624 | tf_op jit(solution)/shard_map/psum | solution.py:40
  971.6 1.6 convert_element_type.25
  973.2 1.6 convert_element_type.27
  (1 shorter events, 0.0 us)
Async XLA Ops:
  7.2 617.7 %copy-start = (bf16[48,1024]{1,0:T(8,128)(2,1)S(1)}, bf16[48,1024]{1,0:T(8,128)(2,1)}, u32[]{:S(2)}) copy-start(bf16[48,1024]{1,0:T(8,128)(2,1)} %param.10) | copy-start | bytes 294916
  7.2 801.9 %reduce-scatter.4.cloned.1.call-start = ((), (), s32[]{:S(2)}) async-start(), calls=%async_computation.2 | async-start | bytes 26738688
  624.9 11.2 %copy-start.4 = (bf16[48,1024]{1,0:T(8,128)(2,1)S(1)}, bf16[48,1024]{1,0:T(8,128)(2,1)}, u32[]{:S(2)}) copy-start(bf16[48,1024]{1,0:T(8,128)(2,1)} %param.11) | copy-start | bytes 294916
  652.4 156.7 %copy-start.3 = (bf16[3,128,1024]{2,1,0:T(8,128)(2,1)S(1)}, bf16[3,128,1024]{2,1,0:T(8,128)(2,1)}, u32[]{:S(2)}) copy-start(bf16[3,128,1024]{2,1,0:T(8,128)(2,1)} %param.13) | copy-start | bytes 2359300
  652.4 156.7 %copy-start.5 = (f32[1024]{0:T(1024)S(1)}, f32[1024]{0:T(1024)}, u32[]{:S(2)}) copy-start(f32[1024]{0:T(1024)} %param.12) | copy-start | bytes 12292
  652.5 249.3 %all-gather.2.cloned.1.call-start = ((), (), s32[]{:S(2)}) async-start(), calls=%async_computation.1 | async-start | bytes 13369344 | tf_op jit(solution)/shard_map/all_gather | solution.py:34
  811.9 159.7 %all-reduce.4.cloned.1.call-start = ((), (), s32[]{:S(2)}) async-start(), calls=%async_computation.3 | async-start | bytes 393216 | tf_op jit(solution)/shard_map/psum | solution.py:40
  901.8 8.2 copy-start.1
  910.0 4.1 copy-start.2
Sparse Core Ops, SparseCore 0:
  652.6 156.4 reduce-scatter.3
  812.0 89.7 all-gather.1
  914.3 57.2 all-reduce.3
where the time goes:
time: 984 us; the launch traced here: 981 us
  local copies, waits for them, and re-layouts  596 us (61%)
  waiting for transfers between devices  302 us (31%)
  matrix products  38.8 us (4%)
  other arithmetic  30 us (3%)
  between operations  14.5 us (1%)
    gather x2, local copies, waits for them, and re-layouts, local(): jnp.take(node_table, neighbor_ids.reshape(-1), axis=1)  578 us
    unnamed x4, waiting for transfers between devices  156 us
    all_gather x1, waiting for transfers between devices, local(): piece = lax.all_gather(delta, 'feat', axis=0, tiled=True)  89.7 us
    psum x1, waiting for transfers between devices, local(): lax.psum(grad_a.astype(jnp.bfloat16), 'dp').astype(jnp.float32)  56.2 us
  transfers between devices with their start and end apart: 3, of which 3 were waited for; matrix products, arithmetic and copies ran while one was open for 0% of the time, Pallas kernels for 0%

commit v1 on v0

v1 whole, which is shorter than its diff:
```python
import jax
import jax.numpy as jnp
from jax import lax
from jax.experimental import pallas as pl
from jax.experimental.pallas import tpu as pltpu
from jax.sharding import PartitionSpec as P

MESH = pl.DeviceIdType.MESH
UNROLL = 8
BATCH = 8


def gather_kernel(counts, ids_hbm, table, out, nodes, sums, *rest):
    fan = ids_hbm.shape[1]
    ids, sem = (rest[:fan], rest[fan : 2 * fan]), rest[2 * fan]
    block, count = table.shape
    tiles, rows = ids_hbm.shape[0], ids_hbm.shape[2]
    chunk = 512

    def fetch(batch, slot, k):
        return pltpu.make_async_copy(
            ids_hbm.at[pl.ds(batch * BATCH, BATCH), k], ids[slot][k], sem.at[slot, k]
        )

    for k in range(fan):
        fetch(0, 0, k).start()

    def fill(i, carry):
        at = pl.multiple_of(i * chunk, chunk)
        part = table[:, pl.ds(at, chunk)]
        wide = jnp.concatenate([part, part, jnp.zeros((128 - 2 * block, chunk), part.dtype)], 0)
        nodes[pl.ds(at, chunk), :] = wide.T.astype(jnp.float32)
        return carry

    lax.fori_loop(0, count // chunk, fill, 0)
    lane_row = lax.broadcasted_iota(jnp.int32, (1, 128), 1)
    lane = lax.broadcasted_iota(jnp.int32, (rows, 128), 1)

    def one_batch(batch, slot):
        def tile(j, carry):
            t = batch * BATCH + j
            live = lax.rem(t, 3) < counts[lax.div(t, 3)]
            at = pl.multiple_of(lax.rem(t, 3) * rows, rows)

            @pl.when(live)
            def _():
                def group(g, inner):
                    for u in range(UNROLL):
                        r = g * UNROLL + u

                        def node(k):
                            return nodes[pl.ds(ids[slot][k][j, r], 1), :]

                        total = node(1)
                        for k in range(2, fan):
                            total = total + node(k)
                        sums[pl.ds(r, 1), :] = jnp.where(lane_row < block, node(0), total)
                    return inner

                lax.fori_loop(0, rows // UNROLL, group, 0)
                held = sums[...]
                held = jnp.where(lane < block, held, held / (fan - 1.0))
                out[lax.div(t, 3), :, pl.ds(at, rows)] = held.T[: 2 * block].astype(out.dtype)

            @pl.when(jnp.logical_not(live))
            def _():
                out[lax.div(t, 3), :, pl.ds(at, rows)] = jnp.zeros((2 * block, rows), out.dtype)

            return carry

        lax.fori_loop(0, BATCH, tile, 0)

    batches = tiles // BATCH

    def pair(p, carry):
        for slot in range(2):
            batch = p * 2 + slot
            for k in range(fan):
                fetch(batch, slot, k).wait()
            if slot == 0:
                for k in range(fan):
                    fetch(batch + 1, 1, k).start()
            else:

                @pl.when(batch < batches - 1)
                def _():
                    for k in range(fan):
                        fetch(batch + 1, 0, k).start()

            one_batch(batch, slot)
        return carry

    lax.fori_loop(0, batches // 2, pair, 0)


def gather(counts, ids, table):
    tiles, fan, rows = ids.shape
    block, count = table.shape
    owned = 3
    return pl.pallas_call(
        gather_kernel,
        grid_spec=pltpu.PrefetchScalarGridSpec(
            num_scalar_prefetch=1,
            grid=(),
            in_specs=[pl.BlockSpec(memory_space=pl.ANY), pl.BlockSpec(memory_space=pltpu.VMEM)],
            out_specs=pl.BlockSpec(memory_space=pltpu.VMEM),
            scratch_shapes=[
                pltpu.VMEM((count, 128), jnp.float32),
                pltpu.VMEM((rows, 128), jnp.float32),
            ]
            + [pltpu.SMEM((BATCH, rows), jnp.int32)] * (2 * fan)
            + [pltpu.SemaphoreType.DMA((2, fan))],
        ),
        out_shape=jax.ShapeDtypeStruct((tiles // owned, 2 * block, owned * rows), jnp.bfloat16),
        compiler_params=pltpu.CompilerParams(vmem_limit_bytes=56 << 20),
        cost_estimate=pl.CostEstimate(
            flops=120_000_000_000, bytes_accessed=300_000_000, transcendentals=0
        ),
    )(counts, ids, table)


def layer_kernel(
    live_count, x, w, bias, cot, act, out_self, out_neigh,
    mine, turned, delta, other, pair_in, summed, feat_in, y_in, half, half_in,
    x_send, x_recv, p_send, p_recv, f_send, f_recv, y_send, y_recv, h_send, h_recv, local_sem,
):
    f, d = lax.axis_index("feat"), lax.axis_index("dp")
    z, xx = lax.div(f, 4), lax.rem(f, 4)
    y, core = lax.div(d, 2), lax.rem(d, 2)
    partner = {"dp": y * 2 + (1 - core)}
    wide, rows = mine.shape
    two = x.shape[1]
    block = two // 2
    hidden = w.shape[1]
    cols = hidden // 2

    def feat_peer(i, j):
        return lax.rem(z + i, 4) * 4 + lax.rem(xx + j, 4)

    def y_peer(i):
        return {"dp": lax.rem(y + i, 4) * 2 + core}

    others = [(i, j) for i in range(4) for j in range(4) if (i, j) != (0, 0)]

    barrier = pltpu.get_barrier_semaphore()
    for i, j in others:
        pl.semaphore_signal(barrier, inc=1, device_id={"feat": feat_peer(i, j)}, device_id_type=MESH)
    pl.semaphore_signal(barrier, inc=1, device_id=partner, device_id_type=MESH)
    for i in range(1, 4):
        pl.semaphore_signal(barrier, inc=1, device_id=y_peer(i), device_id_type=MESH)
    pl.semaphore_wait(barrier, 19)

    my_rows = pl.ds(pl.multiple_of(f * two, two), two)
    own = pltpu.make_async_copy(x.at[f], mine.at[my_rows], local_sem)
    own.start()
    sends = []
    for i, j in others:
        copy = pltpu.make_async_remote_copy(
            src_ref=x.at[feat_peer(i, j)],
            dst_ref=mine.at[my_rows],
            send_sem=x_send.at[i * 4 + j],
            recv_sem=x_recv.at[i * 4 + j],
            device_id={"feat": feat_peer(i, j)},
            device_id_type=MESH,
        )
        copy.start()
        sends.append(copy)
    own.wait()
    for copy in sends:
        copy.wait()

    def turn(i, carry):
        at = pl.multiple_of(i * 128, 128)
        turned[:, pl.ds(at, 128)] = mine[pl.ds(at, 128), :].T
        return carry

    lax.fori_loop(0, wide // 128, turn, 0)

    tile_rows = rows // 3
    tile_of = lax.div(lax.broadcasted_iota(jnp.int32, (rows, 256), 0), tile_rows)
    live = tile_of < live_count[0]

    def forward(n, carry):
        at = pl.multiple_of(n * 256, 256)
        pre = jnp.dot(turned[...], w[:, pl.ds(at, 256)], preferred_element_type=jnp.float32)
        pre = pre + bias[:, pl.ds(at, 256)]
        on = live & (pre > 0)
        act[:, pl.ds(at, 256)] = jnp.where(on, pre, 0.0).astype(act.dtype)
        c = cot[:, pl.ds(at, 256)].astype(jnp.float32)
        delta[:, pl.ds(at, 256)] = jnp.where(on, c, 0.0).astype(delta.dtype)
        return carry

    lax.fori_loop(0, hidden // 256, forward, 0)

    ours = pl.ds(pl.multiple_of(core * cols, cols), cols)
    theirs = pl.ds(pl.multiple_of((1 - core) * cols, cols), cols)
    group = 4 * two

    def rows_of(i):
        return pl.ds(pl.multiple_of(lax.rem(z + i, 4) * group, group), group)

    order = (1, 2, 3, 0)
    waiting = []
    for i in order:
        other[rows_of(i), :] = jnp.dot(
            mine[rows_of(i), :], delta[:, theirs], preferred_element_type=jnp.float32
        ).astype(other.dtype)
        copy = pltpu.make_async_remote_copy(
            src_ref=other.at[rows_of(i)],
            dst_ref=pair_in.at[rows_of(i)],
            send_sem=p_send.at[i],
            recv_sem=p_recv.at[i],
            device_id=partner,
            device_id_type=MESH,
        )
        copy.start()
        waiting.append(copy)
    out_feat = []
    for i, copy in zip(order, waiting):
        product = jnp.dot(mine[rows_of(i), :], delta[:, ours], preferred_element_type=jnp.float32)
        copy.wait()
        summed[rows_of(i), :] = (product + pair_in[rows_of(i), :].astype(jnp.float32)).astype(
            summed.dtype
        )
        for j in (1, 2, 3, 0):
            if (i, j) == (0, 0):
                continue
            peer = feat_peer(i, j)
            send = pltpu.make_async_remote_copy(
                src_ref=summed.at[pl.ds(pl.multiple_of(peer * two, two), two)],
                dst_ref=feat_in.at[i * 4 + j],
                send_sem=f_send.at[i * 4 + j],
                recv_sem=f_recv.at[i * 4 + j],
                device_id={"feat": peer},
                device_id_type=MESH,
            )
            send.start()
            out_feat.append((i * 4 + j, send))
    total = summed[my_rows, :].astype(jnp.float32)
    for slot, send in out_feat:
        send.wait()
        total = total + feat_in[slot].astype(jnp.float32)
    y_in[y] = total.astype(y_in.dtype)
    out_y = []
    for i in range(1, 4):
        send = pltpu.make_async_remote_copy(
            src_ref=y_in.at[y],
            dst_ref=y_in.at[y],
            send_sem=y_send.at[i],
            recv_sem=y_recv.at[i],
            device_id=y_peer(i),
            device_id_type=MESH,
        )
        send.start()
        out_y.append(send)
    for send in out_y:
        send.wait()
    total = y_in[0].astype(jnp.float32)
    for i in range(1, 4):
        total = total + y_in[i].astype(jnp.float32)
    half[...] = total
    last = pltpu.make_async_remote_copy(
        src_ref=half, dst_ref=half_in, send_sem=h_send, recv_sem=h_recv,
        device_id=partner, device_id_type=MESH,
    )
    last.start()
    out_self[:, ours] = total[:block]
    out_neigh[:, ours] = total[block:]
    last.wait()
    out_self[:, theirs] = half_in[:block]
    out_neigh[:, theirs] = half_in[block:]


def layer(count, x, w, bias, cot):
    peers, two, rows = x.shape
    wide, hidden = w.shape
    block, cols = two // 2, hidden // 2
    bf16, f32 = jnp.bfloat16, jnp.float32
    vmem = pl.BlockSpec(memory_space=pltpu.VMEM)
    dma = pltpu.SemaphoreType.DMA
    return pl.pallas_call(
        layer_kernel,
        in_specs=[
            pl.BlockSpec(memory_space=pltpu.SMEM),
            pl.BlockSpec(memory_space=pl.ANY),
            vmem, vmem, vmem,
        ],
        out_specs=[vmem, vmem, vmem],
        out_shape=[
            jax.ShapeDtypeStruct((rows, hidden), bf16),
            jax.ShapeDtypeStruct((block, hidden), f32),
            jax.ShapeDtypeStruct((block, hidden), f32),
        ],
        scratch_shapes=[
            pltpu.VMEM((wide, rows), bf16),
            pltpu.VMEM((rows, wide), bf16),
            pltpu.VMEM((rows, hidden), bf16),
            pltpu.VMEM((wide, cols), bf16),
            pltpu.VMEM((wide, cols), bf16),
            pltpu.VMEM((wide, cols), bf16),
            pltpu.VMEM((peers, two, cols), bf16),
            pltpu.VMEM((4, two, cols), bf16),
            pltpu.VMEM((two, cols), f32),
            pltpu.VMEM((two, cols), f32),
            dma((16,)), dma((16,)), dma((4,)), dma((4,)), dma((16,)), dma((16,)),
            dma((4,)), dma((4,)), dma, dma, dma,
        ],
        compiler_params=pltpu.CompilerParams(
            collective_id=0, has_side_effects=True, vmem_limit_bytes=56 << 20
        ),
        cost_estimate=pl.CostEstimate(
            flops=2_500_000_000, bytes_accessed=10_000_000, transcendentals=0
        ),
    )(count, x, w, bias, cot)


def local(node_table, neighbor_ids, tile_counts, w_self, w_neigh, bias, cotangent):
    owned, rows, hidden = cotangent.shape
    counts = lax.all_gather(tile_counts, "feat", axis=0, tiled=True)
    w = lax.all_gather(jnp.concatenate([w_self, w_neigh], 0), "feat", axis=0, tiled=True)
    x = gather(counts, neighbor_ids, node_table)
    act, grad_self, grad_neigh = layer(
        tile_counts, x, w, bias.reshape(1, hidden), cotangent.reshape(owned * rows, hidden)
    )
    return act.reshape(owned, rows, hidden), grad_self, grad_neigh


def solution(mesh):
    return jax.shard_map(
        local,
        mesh=mesh,
        in_specs=(
            P("feat", None),
            P("dp", None, None),
            P(("dp", "feat")),
            P("feat", None),
            P("feat", None),
            P(),
            P(("dp", "feat"), None, None),
        ),
        out_specs=(P(("dp", "feat"), None, None), P("feat", None), P("feat", None)),
        check_vma=False,
    )
```

time: 984 us -> 212 us (0.22)
  local copies, waits for them, and re-layouts: 596 us -> 9.47 us
  waiting for transfers between devices: 302 us -> 0.04 us
  Pallas kernels: 0 us -> 170 us
  matrix products: 38.8 us -> 0 us
  other arithmetic: 30 us -> 1.63 us
  blocking collectives: 0 us -> 15.2 us
    gather x2 -> x0, local copies, waits for them, and re-layouts: 578 us -> none  [local(): jnp.take(node_table, neighbor_ids.reshape(-1), axis=1)]
    pallas_call x0 -> x2, Pallas kernels: none -> 170 us  [the longest x1 92.4 us: gather(): pl.pallas_call(gather_kernel, grid_spec=pltpu.PrefetchScalarGridSpec(num_...]
    unnamed x4 -> x1, waiting for transfers between devices: 156 us -> 0.02 us
    all_gather x1, waiting for transfers between devices: 89.7 us -> 0.02 us  [local(): lax.all_gather(jnp.concatenate([w_self, w_neigh], 0), 'feat', axis=0, til...]
    psum x1 -> x0, waiting for transfers between devices: 56.2 us -> none  [local(): lax.psum(grad_a.astype(jnp.bfloat16), 'dp').astype(jnp.float32)]
    dot_general x4 -> x0, matrix products: 38.8 us -> none  [the longest x1 16.3 us: local(): jnp.einsum('ftr,fh->trh', mean_part, w_neigh, preferred_element_type=jnp....]
    select_n x3 -> x0, other arithmetic: 16.9 us -> none  [the longest x2 14.2 us: local(): jnp.take(node_table, neighbor_ids.reshape(-1), axis=1)]
    unnamed x0 -> x1, blocking collectives: none -> 15.2 us
  transfers between devices with their start and end apart: 3 -> 1, of which waited for: 3 -> 0; matrix products, arithmetic and copies ran while one was open for 0% -> 1% of each run, Pallas kernels for 0% -> 44%
where the time goes in v1:
time: 212 us
  Pallas kernels  170 us (80%)
  blocking collectives  15.2 us (7%)
  between operations  14.7 us (7%)
  local copies, waits for them, and re-layouts  9.47 us (4%)
    pallas_call x1, Pallas kernels, gather(): pl.pallas_call(gather_kernel, grid_spec=pltpu.PrefetchScalarGridSpec(num_...  92.4 us
    pallas_call x1, Pallas kernels, layer(): pl.pallas_call(layer_kernel, in_specs=[pl.BlockSpec(memory_space=pltpu.SM...  78.1 us
    unnamed x1, blocking collectives  15.2 us
    unnamed x7, local copies, waits for them, and re-layouts  9.47 us
  transfers between devices with their start and end apart: 1, of which 0 were waited for; matrix products, arithmetic and copies ran while one was open for 1% of the time, Pallas kernels for 44%

profile of v1, /device:TPU:1, one launch (start us, length us, event | category | flops | bytes accessed | tf_op | source)
XLA Modules:
  0.0 211.5 jit_solution(5411261473594433384)
XLA Ops:
  7.2 0.0 all-gather.2.cloned.1.call-start
  7.9 1.2 dynamic-slice
  9.1 1.6 pad_maximum_fusion
  10.7 0.8 dynamic-update-slice
  11.5 0.0 all-gather.2.cloned.1.call-update
  11.5 15.2 %all-reduce.counts = s32[16]{0:T(128)} all-reduce(s32[16]{0:T(128)S(1)} %dynamic-update-slice), channel_id=1, replica_groups=mesh['feat'=16,'dp'=8] {'feat'}, use_global_device_ids=true, to_apply=%add | all-reduce | flops 16 | bytes 128
  26.7 2.2 %copy.10.ids_hbm = s32[48,26,128]{2,1,0:T(8,128)} copy(s32[48,26,128]{2,0,1:T(8,128)} %param.8) | data formatting | bytes 1277952 | tf_op args[1]
  28.8 92.4 %shard_map.94.x = bf16[16,96,384]{2,1,0:T(8,128)(2,1)} custom-call(s32[16]{0:T(128)} %all-reduce.counts, s32[48,26,128]{2,1,0:T(8,128)} %copy.10.ids_hbm, bf16[48,65536]{1,0:T(8,128)(2,1)} %table.1), custom_call_target="tpu_custom_call" | custom-call | flops 120000004096 | bytes 300000000 | tf_op jit(solution)/shard_map/pallas_call | solution.py:100
  121.3 0.0 all-gather.2.cloned.1.call-done.w
  121.3 78.1 %shard_map.95 = (bf16[384,1024]{1,0:T(8,128)(2,1)}, f32[48,1024]{1,0:T(8,128)}, f32[48,1024]{1,0:T(8,128)}) custom-call(s32[1]{0:T(128)S(6)} %copy.15.live_count, bf16[16,96,384]{2,1,0:T(8,128)(2,1)} %shard_map.94.x, bf16[1536,1024]{1,0:T(8,128)(2,1)} %all-gather.2.cloned.1.call-done.w, f32[1,1024]{1,0:T(1,128)} %bitcast.6, bf16[384,1024]{1,0:T(8,128)(2,1)} %bitcast.5), custom_call_target="tpu_custom_call" | custom-call | flops 2500000000 | bytes 10000000 | tf_op jit(solution)/shard_map/pallas_call | solution.py:281
  199.4 2.1 copy.16
  201.4 1.6 copy.17
  203.1 1.6 copy.18
  (1 shorter events, 0.0 us)
Async XLA Ops:
  7.2 114.1 %all-gather.2.cloned.1.call-start = ((), (), s32[]{:S(2)}) async-start(), calls=%async_computation | async-start | bytes 3342336 | tf_op jit(solution)/shard_map/all_gather | solution.py:320
Sparse Core Ops, SparseCore 0:
  11.6 51.0 all-gather.1

commit v2 on v1

v2 whole, which is shorter than its diff:
```python
import jax
import jax.numpy as jnp
from jax import lax
from jax.experimental import pallas as pl
from jax.experimental.pallas import tpu as pltpu
from jax.sharding import PartitionSpec as P

MESH = pl.DeviceIdType.MESH
UNROLL = 16
BATCH = 8
CHUNK = 2048
LOADS = 8


def gather_kernel(counts, ids_hbm, table_hbm, out, nodes, sums, table, load_sem, *rest):
    fan, tiles, rows = ids_hbm.shape
    ids, sem = (rest[:fan], rest[fan : 2 * fan]), rest[2 * fan]
    block, count = table_hbm.shape
    piece = count // LOADS

    def load(i):
        at = pl.ds(pl.multiple_of(i * piece, piece), piece)
        return pltpu.make_async_copy(table_hbm.at[:, at], table.at[:, at], load_sem.at[i])

    for i in range(LOADS):
        load(i).start()

    def fetch(batch, slot, k):
        return pltpu.make_async_copy(
            ids_hbm.at[k, pl.ds(batch * BATCH, BATCH)], ids[slot][k], sem.at[slot, k]
        )

    for k in range(fan):
        fetch(0, 0, k).start()

    def fill(i, carry):
        load(i).wait()

        def turn(j, inner):
            at = pl.multiple_of(i * piece + j * CHUNK, CHUNK)
            part = table[:, pl.ds(at, CHUNK)]
            wide = jnp.concatenate([part, part, jnp.zeros((128 - 2 * block, CHUNK), part.dtype)], 0)
            nodes[pl.ds(at, CHUNK), :] = wide.T.astype(jnp.float32)
            return inner

        lax.fori_loop(0, piece // CHUNK, turn, 0)
        return carry

    lax.fori_loop(0, LOADS, fill, 0)
    lane_row = lax.broadcasted_iota(jnp.int32, (1, 128), 1)
    lane = lax.broadcasted_iota(jnp.int32, (rows, 128), 1)

    def one_batch(batch, slot):
        def tile(j, carry):
            t = batch * BATCH + j
            live = lax.rem(t, 3) < counts[lax.div(t, 3), 0, 0]
            at = pl.multiple_of(lax.rem(t, 3) * rows, rows)

            @pl.when(live)
            def _():
                def group(g, inner):
                    for u in range(UNROLL):
                        r = g * UNROLL + u

                        def node(k):
                            return nodes[pl.ds(ids[slot][k][j, r], 1), :]

                        total = node(1)
                        for k in range(2, fan):
                            total = total + node(k)
                        sums[pl.ds(r, 1), :] = jnp.where(lane_row < block, node(0), total)
                    return inner

                lax.fori_loop(0, rows // UNROLL, group, 0)
                held = sums[...]
                held = jnp.where(lane < block, held, held / (fan - 1.0))
                turned = held.T.astype(out.dtype)
                out[lax.div(t, 3), 0, :, pl.ds(at, rows)] = turned[:block]
                out[lax.div(t, 3), 1, :, pl.ds(at, rows)] = turned[block : 2 * block]

            @pl.when(jnp.logical_not(live))
            def _():
                out[lax.div(t, 3), :, :, pl.ds(at, rows)] = jnp.zeros((2, block, rows), out.dtype)

            return carry

        lax.fori_loop(0, BATCH, tile, 0)

    batches = tiles // BATCH

    def pair(p, carry):
        for slot in range(2):
            batch = p * 2 + slot
            for k in range(fan):
                fetch(batch, slot, k).wait()
            if slot == 0:
                for k in range(fan):
                    fetch(batch + 1, 1, k).start()
            else:

                @pl.when(batch < batches - 1)
                def _():
                    for k in range(fan):
                        fetch(batch + 1, 0, k).start()

            one_batch(batch, slot)
        return carry

    lax.fori_loop(0, batches // 2, pair, 0)


def gather(counts, ids, table):
    fan, tiles, rows = ids.shape
    block, count = table.shape
    owned = 3
    return pl.pallas_call(
        gather_kernel,
        in_specs=[
            pl.BlockSpec(memory_space=pltpu.SMEM),
            pl.BlockSpec(memory_space=pl.ANY),
            pl.BlockSpec(memory_space=pl.ANY),
        ],
        out_specs=pl.BlockSpec(memory_space=pltpu.VMEM),
        scratch_shapes=[
            pltpu.VMEM((count, 128), jnp.float32),
            pltpu.VMEM((rows, 128), jnp.float32),
            pltpu.VMEM((block, count), table.dtype),
            pltpu.SemaphoreType.DMA((LOADS,)),
        ]
        + [pltpu.SMEM((BATCH, rows), jnp.int32)] * (2 * fan)
        + [pltpu.SemaphoreType.DMA((2, fan))],
        out_shape=jax.ShapeDtypeStruct((tiles // owned, 2, block, owned * rows), jnp.bfloat16),
        compiler_params=pltpu.CompilerParams(vmem_limit_bytes=56 << 20),
        cost_estimate=pl.CostEstimate(
            flops=120_000_000_000, bytes_accessed=300_000_000, transcendentals=0
        ),
    )(counts, ids, table)


def count_kernel(count, out, got, send_sem, recv_sem):
    f = lax.axis_index("feat")
    peers = out.shape[0]
    barrier = pltpu.get_barrier_semaphore()
    for i in range(1, peers):
        pl.semaphore_signal(
            barrier, inc=1, device_id={"feat": lax.rem(f + i, peers)}, device_id_type=MESH
        )
    got[f] = jnp.zeros(got.shape[1:], jnp.int32) + count[0]
    pl.semaphore_wait(barrier, peers - 1)
    copies = []
    for i in range(1, peers):
        copy = pltpu.make_async_remote_copy(
            src_ref=got.at[f],
            dst_ref=got.at[f],
            send_sem=send_sem.at[i],
            recv_sem=recv_sem.at[i],
            device_id={"feat": lax.rem(f + i, peers)},
            device_id_type=MESH,
        )
        copy.start()
        copies.append(copy)
    for copy in copies:
        copy.wait()
    out[...] = got[...]


def exchange_counts(count):
    peers = 16
    return pl.pallas_call(
        count_kernel,
        in_specs=[pl.BlockSpec(memory_space=pltpu.SMEM)],
        out_specs=pl.BlockSpec(memory_space=pltpu.VMEM),
        out_shape=jax.ShapeDtypeStruct((peers, 1, 128), jnp.int32),
        scratch_shapes=[
            pltpu.VMEM((peers, 1, 128), jnp.int32),
            pltpu.SemaphoreType.DMA((peers,)),
            pltpu.SemaphoreType.DMA((peers,)),
        ],
        compiler_params=pltpu.CompilerParams(collective_id=1, has_side_effects=True),
    )(count)


def finish_kernel(a, b, c, out_a, out_b, out_c, sem):
    copies = [
        pltpu.make_async_copy(x, y, sem.at[i])
        for i, (x, y) in enumerate(((a, out_a), (b, out_b), (c, out_c)))
    ]
    for copy in copies:
        copy.start()
    for copy in copies:
        copy.wait()


def finish(*arrays):
    return pl.pallas_call(
        finish_kernel,
        in_specs=[pl.BlockSpec(memory_space=pl.ANY)] * 3,
        out_specs=[pl.BlockSpec(memory_space=pl.ANY)] * 3,
        out_shape=[jax.ShapeDtypeStruct(x.shape, x.dtype) for x in arrays],
        scratch_shapes=[pltpu.SemaphoreType.DMA((3,))],
        compiler_params=pltpu.CompilerParams(vmem_limit_bytes=56 << 20),
    )(*arrays)


def layer_kernel(
    live_count, x, w_self, w_neigh, bias, cot, act, out_self, out_neigh,
    w, mine, turned, delta, other, pair_in, part_a, relay_a, in_a, part_b, relay_b, in_b,
    y_out, y_in, half, half_in, x_send, x_recv, p_send, p_recv, r_send, r_recv, y_send, y_recv, h_send, h_recv, local_sem, w_sem,
):
    f, d = lax.axis_index("feat"), lax.axis_index("dp")
    z, xx = lax.div(f, 4), lax.rem(f, 4)
    y, core = lax.div(d, 2), lax.rem(d, 2)
    partner = {"dp": y * 2 + (1 - core)}
    half_wide, rows = mine.shape[1:]
    block = x.shape[2]
    hidden = w.shape[1]
    cols = hidden // 2

    def feat_peer(i, j):
        return lax.rem(z + i, 4) * 4 + lax.rem(xx + j, 4)

    others = [(i, j) for i in range(4) for j in range(4) if (i, j) != (0, 0)]

    weights = [
        pltpu.make_async_copy(part, w.at[pl.ds(p * half_wide, half_wide)], w_sem.at[p])
        for p, part in enumerate((w_self, w_neigh))
    ]
    for copy in weights:
        copy.start()

    barrier = pltpu.get_barrier_semaphore()
    for i, j in others:
        pl.semaphore_signal(barrier, inc=1, device_id={"feat": feat_peer(i, j)}, device_id_type=MESH)
    pl.semaphore_signal(barrier, inc=1, device_id=partner, device_id_type=MESH)
    for at in (y + 1 - 2 * lax.rem(y, 2), 3 - y):
        pl.semaphore_signal(barrier, inc=1, device_id={"dp": at * 2 + core}, device_id_type=MESH)
    pl.semaphore_wait(barrier, 18)

    my_rows = pl.ds(pl.multiple_of(f * block, block), block)
    own = pltpu.make_async_copy(x.at[f], mine.at[:, my_rows], local_sem)
    own.start()
    sends = []
    for i, j in others:
        copy = pltpu.make_async_remote_copy(
            src_ref=x.at[feat_peer(i, j)],
            dst_ref=mine.at[:, my_rows],
            send_sem=x_send.at[i * 4 + j],
            recv_sem=x_recv.at[i * 4 + j],
            device_id={"feat": feat_peer(i, j)},
            device_id_type=MESH,
        )
        copy.start()
        sends.append(copy)
    own.wait()
    for copy in sends:
        copy.wait()

    def turn(i, carry):
        at = pl.multiple_of(i * 128, 128)
        for p in range(2):
            to = pl.multiple_of(p * half_wide + i * 128, 128)
            turned[:, pl.ds(to, 128)] = mine[p, pl.ds(at, 128), :].T
        return carry

    lax.fori_loop(0, half_wide // 128, turn, 0)
    for copy in weights:
        copy.wait()

    tile_rows = rows // 3
    tile_of = lax.div(lax.broadcasted_iota(jnp.int32, (rows, 256), 0), tile_rows)
    live = tile_of < live_count[0]

    def forward(n, carry):
        at = pl.multiple_of(n * 256, 256)
        pre = jnp.dot(turned[...], w[:, pl.ds(at, 256)], preferred_element_type=jnp.float32)
        pre = pre + bias[:, pl.ds(at, 256)]
        on = live & (pre > 0)
        act[:, pl.ds(at, 256)] = jnp.where(on, pre, 0.0).astype(act.dtype)
        c = cot[:, pl.ds(at, 256)].astype(jnp.float32)
        delta[:, pl.ds(at, 256)] = jnp.where(on, c, 0.0).astype(delta.dtype)
        return carry

    lax.fori_loop(0, hidden // 256, forward, 0)

    quarter = cols // 2

    def ours(h):
        return pl.ds(pl.multiple_of(core * cols + h * quarter, quarter), quarter)

    def theirs(h):
        return pl.ds(pl.multiple_of((1 - core) * cols + h * quarter, quarter), quarter)

    def product(p, at):
        return jnp.dot(mine[p], delta[:, at], preferred_element_type=jnp.float32)

    def remote(src, dst, send_sem, recv_sem, peer):
        copy = pltpu.make_async_remote_copy(
            src_ref=src, dst_ref=dst, send_sem=send_sem, recv_sem=recv_sem,
            device_id=peer, device_id_type=MESH,
        )
        copy.start()
        return copy

    def place(h, phase):
        return xx if (h + phase) % 2 == 0 else z

    def neighbour(h, phase, s):
        at = lax.rem(place(h, phase) + 4 + s, 4)
        return {"feat": z * 4 + at if (h + phase) % 2 == 0 else at * 4 + xx}

    phases = ((part_a, relay_a, in_a), (part_b, relay_b, in_b))
    started = {}

    def ring(h, phase, messages):
        part, relay, arrived = (buffer.at[h] for buffer in phases[phase])
        pos = place(h, phase)
        far, after, before = (lax.rem(pos + s, 4) for s in (2, 1, 3))
        plan = (
            (1, part.at[far, 0], relay.at[0]),
            (-1, part.at[far, 1], relay.at[1]),
            (1, part.at[after, 1], arrived.at[0, 1]),
            (-1, part.at[before, 0], arrived.at[1, 0]),
            (1, part.at[after, 0], arrived.at[0, 0]),
            (-1, part.at[before, 1], arrived.at[1, 1]),
        )
        for m in messages:
            step, src, dst = plan[m]
            started[h, phase, m] = remote(
                src, dst, r_send.at[phase, h, m], r_recv.at[phase, h, m], neighbour(h, phase, step)
            )

    def pass_on(h, phase):
        part, relay, _ = (buffer.at[h] for buffer in phases[phase])
        pos = place(h, phase)
        for way, step in ((0, 1), (1, 3)):
            at = lax.rem(pos + step, 4)
            started[h, phase, way].wait_recv()
            part[at, way] = (
                part[at, way].astype(jnp.float32) + relay[way].astype(jnp.float32)
            ).astype(part.dtype)
            ring(h, phase, (4 + way,))

    def gathered(h, phase, p):
        part, _, arrived = (buffer.at[h] for buffer in phases[phase])
        for m in ((4, 3), (2, 5))[p]:
            started[h, phase, m].wait_recv()
        return (
            part[place(h, phase), p].astype(jnp.float32)
            + arrived[0, p].astype(jnp.float32)
            + arrived[1, p].astype(jnp.float32)
        )

    order = ((0, 0), (0, 1), (1, 0), (1, 1))
    pairs = []
    for q, (h, p) in enumerate(order):
        other[q] = product(p, theirs(h)).astype(other.dtype)
        pairs.append(remote(other.at[q], pair_in.at[q], p_send.at[q], p_recv.at[q], partner))
    for q, (h, p) in enumerate(order):
        own_part = product(p, ours(h))
        pairs[q].wait_recv()
        own_part = (own_part + pair_in[q].astype(jnp.float32)).astype(part_a.dtype)
        for i in range(4):
            for j in range(4):
                rows_ij = own_part[(i * 4 + j) * block : (i * 4 + j + 1) * block]
                if h == 0:
                    part_a[h, j, p, i] = rows_ij
                else:
                    part_a[h, i, p, j] = rows_ij
        ring(h, 0, (0, 3) if p == 0 else (1, 2))
        if q >= 2:
            pass_on(q - 2, 0)
    for h in range(2):
        for p in range(2):
            reduced = gathered(h, 0, p).astype(part_b.dtype)
            for i in range(4):
                part_b[h, i, p] = reduced[i]
            ring(h, 1, (0, 3) if p == 0 else (1, 2))
    for h in range(2):
        pass_on(h, 1)

    def y_peer_of(h, stage):
        at = y + 1 - 2 * lax.rem(y, 2) if (h + stage) % 2 == 0 else 3 - y
        return {"dp": at * 2 + core}

    across = {}
    for h in range(2):
        for p in range(2):
            y_out[h, 0, p] = gathered(h, 1, p).astype(y_out.dtype)
        across[h, 0] = remote(
            y_out.at[h, 0], y_in.at[h, 0], y_send.at[h, 0], y_recv.at[h, 0], y_peer_of(h, 0)
        )
    for h in range(2):
        across[h, 0].wait_recv()
        both = y_out[h, 0].astype(jnp.float32) + y_in[h, 0].astype(jnp.float32)
        y_out[h, 1] = both.astype(y_out.dtype)
        across[h, 1] = remote(
            y_out.at[h, 1], y_in.at[h, 1], y_send.at[h, 1], y_recv.at[h, 1], y_peer_of(h, 1)
        )
    last = []
    for h in range(2):
        across[h, 1].wait_recv()
        half[h] = y_out[h, 1].astype(jnp.float32) + y_in[h, 1].astype(jnp.float32)
        last.append(remote(half.at[h], half_in.at[h], h_send.at[h], h_recv.at[h], partner))
        out_self[:, ours(h)] = half[h, 0]
        out_neigh[:, ours(h)] = half[h, 1]
    for h in range(2):
        last[h].wait_recv()
        out_self[:, theirs(h)] = half_in[h, 0]
        out_neigh[:, theirs(h)] = half_in[h, 1]
    for copy in [*pairs, *started.values(), *across.values(), *last]:
        copy.wait_send()


def layer(count, x, w_self, w_neigh, bias, cot):
    peers, _, block, rows = x.shape
    half_wide, hidden = w_self.shape
    quarter = hidden // 4
    bf16, f32 = jnp.bfloat16, jnp.float32
    vmem = pl.BlockSpec(memory_space=pltpu.VMEM)
    hbm = pl.BlockSpec(memory_space=pl.ANY)
    dma = pltpu.SemaphoreType.DMA
    return pl.pallas_call(
        layer_kernel,
        in_specs=[pl.BlockSpec(memory_space=pltpu.SMEM), hbm, hbm, hbm, vmem, vmem],
        out_specs=[vmem, vmem, vmem],
        out_shape=[
            jax.ShapeDtypeStruct((rows, hidden), bf16),
            jax.ShapeDtypeStruct((block, hidden), f32),
            jax.ShapeDtypeStruct((block, hidden), f32),
        ],
        scratch_shapes=[
            pltpu.VMEM((2 * half_wide, hidden), bf16),
            pltpu.VMEM((2, half_wide, rows), bf16),
            pltpu.VMEM((rows, 2 * half_wide), bf16),
            pltpu.VMEM((rows, hidden), bf16),
            pltpu.VMEM((4, half_wide, quarter), bf16),
            pltpu.VMEM((4, half_wide, quarter), bf16),
            pltpu.VMEM((2, 4, 2, 4, block, quarter), bf16),
            pltpu.VMEM((2, 2, 4, block, quarter), bf16),
            pltpu.VMEM((2, 2, 2, 4, block, quarter), bf16),
            pltpu.VMEM((2, 4, 2, block, quarter), bf16),
            pltpu.VMEM((2, 2, block, quarter), bf16),
            pltpu.VMEM((2, 2, 2, block, quarter), bf16),
            pltpu.VMEM((2, 2, 2, block, quarter), bf16),
            pltpu.VMEM((2, 2, 2, block, quarter), bf16),
            pltpu.VMEM((2, 2, block, quarter), f32),
            pltpu.VMEM((2, 2, block, quarter), f32),
            dma((16,)), dma((16,)), dma((4,)), dma((4,)), dma((2, 2, 6)), dma((2, 2, 6)),
            dma((2, 2)), dma((2, 2)), dma((2,)), dma((2,)), dma, dma((2,)),
        ],
        compiler_params=pltpu.CompilerParams(
            collective_id=0, has_side_effects=True, vmem_limit_bytes=56 << 20
        ),
        cost_estimate=pl.CostEstimate(
            flops=2_500_000_000, bytes_accessed=10_000_000, transcendentals=0
        ),
    )(count, x, w_self, w_neigh, bias, cot)


def local(node_table, neighbor_ids, tile_counts, w_self, w_neigh, bias, cotangent):
    owned, rows, hidden = cotangent.shape
    w_self_all = lax.all_gather(w_self, "feat", axis=0, tiled=True)
    w_neigh_all = lax.all_gather(w_neigh, "feat", axis=0, tiled=True)
    x = gather(exchange_counts(tile_counts), neighbor_ids.transpose(1, 0, 2), node_table)
    act, grad_self, grad_neigh = layer(
        tile_counts,
        x,
        w_self_all,
        w_neigh_all,
        bias.reshape(1, hidden),
        cotangent.reshape(owned * rows, hidden),
    )
    act, grad_self, grad_neigh = finish(act, grad_self, grad_neigh)
    return act.reshape(owned, rows, hidden), grad_self, grad_neigh


def solution(mesh):
    return jax.shard_map(
        local,
        mesh=mesh,
        in_specs=(
            P("feat", None),
            P("dp", None, None),
            P(("dp", "feat")),
            P("feat", None),
            P("feat", None),
            P(),
            P(("dp", "feat"), None, None),
        ),
        out_specs=(P(("dp", "feat"), None, None), P("feat", None), P("feat", None)),
        check_vma=False,
    )
```

time: 212 us -> 220 us (1.038)
  Pallas kernels: 170 us -> 202 us
  blocking collectives: 15.2 us -> 0 us
  local copies, waits for them, and re-layouts: 9.47 us -> 0 us
    pallas_call x1 -> x3, Pallas kernels: 92.4 us -> 137 us  [the longest x1 89.7 us: gather(): pl.pallas_call(gather_kernel, in_specs=[pl.BlockSpec(memory_space=pltpu.S...]
    unnamed x1 -> x0, blocking collectives: 15.2 us -> none
    pallas_call x1, Pallas kernels: 78.1 us -> 64.3 us  [layer(): pl.pallas_call(layer_kernel, in_specs=[pl.BlockSpec(memory_space=pltpu.SM...]
    unnamed x7 -> x0, local copies, waits for them, and re-layouts: 9.47 us -> none
  transfers between devices with their start and end apart: 1 -> 2, of which waited for: 0 -> 0; matrix products, arithmetic and copies ran while one was open for 1% -> 0% of each run, Pallas kernels for 44% -> 46%
where the time goes in v2:
time: 220 us; the launch traced here: 218 us
  Pallas kernels  202 us (92%)
  between operations  14.7 us (7%)
    pallas_call x1, Pallas kernels, gather(): pl.pallas_call(gather_kernel, in_specs=[pl.BlockSpec(memory_space=pltpu.S...  89.7 us
    pallas_call x1, Pallas kernels, layer(): pl.pallas_call(layer_kernel, in_specs=[pl.BlockSpec(memory_space=pltpu.SM...  64.3 us
    pallas_call x1, Pallas kernels, finish(): pl.pallas_call(finish_kernel, in_specs=[pl.BlockSpec(memory_space=pl.ANY)...  36.9 us
    pallas_call x1, Pallas kernels, exchange_counts(): pl.pallas_call(count_kernel, in_specs=[pl.BlockSpec(memory_space=pltpu.SM...  10.9 us
  transfers between devices with their start and end apart: 2, of which 0 were waited for; matrix products, arithmetic and copies ran while one was open for 0% of the time, Pallas kernels for 46%

profile of v2, /device:TPU:1, one launch (start us, length us, event | category | flops | bytes accessed | tf_op | source)
XLA Modules:
  0.0 218.0 jit_solution(9459987060528031868)
XLA Ops:
  7.2 0.0 all-gather.3.cloned.1.call-start
  7.2 0.7 all-gather.3.cloned.1.call-update
  7.9 0.0 all-gather.5.cloned.1.call-start
  7.9 0.7 all-gather.5.cloned.1.call-update
  9.3 10.9 %shard_map.94.counts = s32[16,1,128]{2,1,0:T(1,128)} custom-call(s32[1]{0:T(128)S(6)} %copy.10.count.live_count), custom_call_target="tpu_custom_call" | custom-call | tf_op jit(solution)/shard_map/pallas_call | solution.py:169
  20.2 89.7 %shard_map.95.x = bf16[16,2,48,384]{3,2,1,0:T(8,128)(2,1)} custom-call(s32[16,1,128]{2,1,0:T(1,128)} %shard_map.94.counts, s32[26,48,128]{2,1,0:T(8,128)} %bitcast.6, bf16[48,65536]{1,0:T(8,128)(2,1)} %table_hbm.1), custom_call_target="tpu_custom_call" | custom-call | flops 120000004096 | bytes 300000000 | tf_op jit(solution)/shard_map/pallas_call | solution.py:116
  109.9 0.0 all-gather.3.cloned.1.call-done.w_self
  109.9 0.0 all-gather.5.cloned.1.call-done.w_neigh
  109.9 64.3 %shard_map.96 = (bf16[384,1024]{1,0:T(8,128)(2,1)}, f32[48,1024]{1,0:T(8,128)}, f32[48,1024]{1,0:T(8,128)}) custom-call(s32[1]{0:T(128)S(6)} %copy.10.count.live_count, bf16[16,2,48,384]{3,2,1,0:T(8,128)(2,1)} %shard_map.95.x, bf16[768,1024]{1,0:T(8,128)(2,1)} %all-gather.3.cloned.1.call-done.w_self, bf16[768,1024]{1,0:T(8,128)(2,1)} %all-gather.5.cloned.1.call-done.w_neigh, ...), custom_call_target="tpu_custom_call" | custom-call | flops 2500000000 | bytes 10000000 | tf_op jit(solution)/shard_map/pallas_call | solution.py:422
  174.3 36.9 %shard_map.97 = (bf16[384,1024]{1,0:T(8,128)(2,1)}, f32[48,1024]{1,0:T(8,128)}, f32[48,1024]{1,0:T(8,128)}) custom-call(bf16[384,1024]{1,0:T(8,128)(2,1)} %get-tuple-element.9.a, f32[48,1024]{1,0:T(8,128)} %get-tuple-element.10.b, f32[48,1024]{1,0:T(8,128)} %get-tuple-element.11.c), custom_call_target="tpu_custom_call" | custom-call | tf_op jit(solution)/shard_map/pallas_call | solution.py:195
Async XLA Ops:
  7.2 102.7 %all-gather.3.cloned.1.call-start = ((), (), s32[]{:S(2)}) async-start(), calls=%async_computation | async-start | bytes 1671168 | tf_op jit(solution)/shard_map/all_gather | solution.py:462
  7.9 102.0 %all-gather.5.cloned.1.call-start = ((), (), s32[]{:S(2)}) async-start(), calls=%async_computation.1 | async-start | bytes 1671168 | tf_op jit(solution)/shard_map/all_gather | solution.py:463
Sparse Core Ops, SparseCore 0:
  10.1 46.3 all-gather.2
  58.6 43.3 all-gather.4

commit v3 on v2

--- a/solution.py
+++ b/solution.py
@@ -12,26 +12,60 @@
 LOADS = 8
 
 
-def gather_kernel(counts, ids_hbm, table_hbm, out, nodes, sums, table, load_sem, *rest):
-    fan, tiles, rows = ids_hbm.shape
-    ids, sem = (rest[:fan], rest[fan : 2 * fan]), rest[2 * fan]
-    block, count = table_hbm.shape
-    piece = count // LOADS
+def tile_sums(nodes, sums, ids, rows, block, base):
+    lane_row = lax.broadcasted_iota(jnp.int32, (1, 128), 1)
+
+    def group(g, carry):
+        for u in range(UNROLL):
+            r = g * UNROLL + u
+
+            def node(k):
+                return nodes[pl.ds(ids[k][base + r], 1), :]
+
+            total = node(1)
+            for k in range(2, len(ids)):
+                total = total + node(k)
+            sums[pl.ds(r, 1), :] = jnp.where(lane_row < block, node(0), total)
+        return carry
+
+    lax.fori_loop(0, rows // UNROLL, group, 0)
+    held = sums[...]
+    lane = lax.broadcasted_iota(jnp.int32, held.shape, 1)
+    held = jnp.where(lane < block, held, held / (len(ids) - 1.0))
+    return held.T.astype(jnp.bfloat16)
+
+
+def first_kernel(
+    count, ids_hbm, table_hbm, nodes, counts, first, table, sums, sent, landed, got, *rest
+):
+    fan, _, rows = ids_hbm.shape
+    ids = (rest[:fan], rest[fan : 2 * fan])
+    ids_sem, load_sem, c_send, c_recv, x_send, x_recv = rest[2 * fan :]
+    block, width = table_hbm.shape
+    peers = got.shape[0]
+    f = lax.axis_index("feat")
+    piece = width // LOADS
 
     def load(i):
         at = pl.ds(pl.multiple_of(i * piece, piece), piece)
         return pltpu.make_async_copy(table_hbm.at[:, at], table.at[:, at], load_sem.at[i])
 
+    def peer(i):
+        return lax.rem(f + i, peers)
+
+    def fetch(i, slot, k):
+        return pltpu.make_async_copy(
+            ids_hbm.at[k, peer(i) * 3], ids[slot][k], ids_sem.at[slot, k]
+        )
+
     for i in range(LOADS):
         load(i).start()
-
-    def fetch(batch, slot, k):
-        return pltpu.make_async_copy(
-            ids_hbm.at[k, pl.ds(batch * BATCH, BATCH)], ids[slot][k], sem.at[slot, k]
-        )
-
     for k in range(fan):
-        fetch(0, 0, k).start()
+        fetch(1, 0, k).start()
+    barrier = pltpu.get_barrier_semaphore()
+    for i in range(1, peers):
+        pl.semaphore_signal(barrier, inc=1, device_id={"feat": peer(i)}, device_id_type=MESH)
+    got[f] = jnp.zeros(got.shape[1:], jnp.int32) + count[0]
 
     def fill(i, carry):
         load(i).wait()
@@ -47,40 +81,130 @@
         return carry
 
     lax.fori_loop(0, LOADS, fill, 0)
-    lane_row = lax.broadcasted_iota(jnp.int32, (1, 128), 1)
-    lane = lax.broadcasted_iota(jnp.int32, (rows, 128), 1)
+    pl.semaphore_wait(barrier, peers - 1)
+
+    def count_copy(i):
+        return pltpu.make_async_remote_copy(
+            src_ref=got.at[f], dst_ref=got.at[f], send_sem=c_send.at[i], recv_sem=c_recv.at[i],
+            device_id={"feat": peer(i)}, device_id_type=MESH,
+        )
+
+    my_rows = pl.ds(pl.multiple_of(f * block, block), block)
+
+    def tile_copy(i):
+        return pltpu.make_async_remote_copy(
+            src_ref=sent.at[peer(i)], dst_ref=landed.at[:, my_rows],
+            send_sem=x_send.at[i], recv_sem=x_recv.at[i],
+            device_id={"feat": peer(i)}, device_id_type=MESH,
+        )
+
+    for i in range(1, peers):
+        count_copy(i).start()
+
+    def pair(p, carry):
+        for slot in range(2):
+            i = p * 2 + slot + 1
+            for k in range(fan):
+                fetch(i, slot, k).wait()
+            if slot == 0:
+                for k in range(fan):
+                    fetch(i + 1, 1, k).start()
+            else:
+
+                @pl.when(i < peers)
+                def _():
+                    for k in range(fan):
+                        fetch(i + 1, 0, k).start()
+
+            turned = tile_sums(nodes, sums, ids[slot], rows, block, 0)
+            for part in range(2):
+                sent[peer(i), part] = turned[part * block : (part + 1) * block]
+
+            @pl.when(i < peers)
+            def _():
+                tile_copy(i).start()
+
+        return carry
+
+    lax.fori_loop(0, peers // 2, pair, 0)
+    for part in range(2):
+        landed[part, my_rows] = sent[f, part]
+
+    def settle(i, carry):
+        count_copy(i).wait()
+        tile_copy(i).wait()
+        return carry
+
+    lax.fori_loop(1, peers, settle, 0)
+    counts[...] = got[...]
+    first[...] = landed[...]
+
+
+def first_tiles(count, ids, table):
+    fan, tiles, rows = ids.shape
+    block, width = table.shape
+    peers = tiles // 3
+    dma = pltpu.SemaphoreType.DMA
+    hbm = pl.BlockSpec(memory_space=pl.ANY)
+    vmem = pl.BlockSpec(memory_space=pltpu.VMEM)
+    nodes, counts, first = pl.pallas_call(
+        first_kernel,
+        in_specs=[pl.BlockSpec(memory_space=pltpu.SMEM), hbm, hbm],
+        out_specs=[vmem, vmem, vmem],
+        out_shape=[
+            pltpu.VMEM((width, 128), jnp.float32),
+            jax.ShapeDtypeStruct((peers, 1, 128), jnp.int32),
+            jax.ShapeDtypeStruct((2, peers * block, rows), jnp.bfloat16),
+        ],
+        scratch_shapes=[
+            pltpu.VMEM((block, width), table.dtype),
+            pltpu.VMEM((rows, 128), jnp.float32),
+            pltpu.VMEM((peers, 2, block, rows), jnp.bfloat16),
+            pltpu.VMEM((2, peers * block, rows), jnp.bfloat16),
+            pltpu.VMEM((peers, 1, 128), jnp.int32),
+        ]
+        + [pltpu.SMEM((rows,), jnp.int32)] * (2 * fan)
+        + [dma((2, fan)), dma((LOADS,)), dma((peers,)), dma((peers,)), dma((peers,)), dma((peers,))],
+        compiler_params=pltpu.CompilerParams(
+            collective_id=1, has_side_effects=True, vmem_limit_bytes=16 << 20
+        ),
+        cost_estimate=pl.CostEstimate(
+            flops=60_000_000_000, bytes_accessed=150_000_000, transcendentals=0
+        ),
+    )(count, ids, table)
+    return pltpu.with_memory_space_constraint(nodes, pltpu.VMEM), counts, first
+
+
+def gather_kernel(counts, ids_hbm, nodes, out, sums, *rest):
+    fan, tiles, rows = ids_hbm.shape
+    ids, sem = (rest[:fan], rest[fan : 2 * fan]), rest[2 * fan]
+    block = out.shape[2]
+    flat = [[ref.reshape(BATCH * rows) for ref in refs] for refs in ids]
+
+    def fetch(batch, slot, k):
+        return pltpu.make_async_copy(
+            ids_hbm.at[k, pl.ds(batch * BATCH, BATCH)], ids[slot][k], sem.at[slot, k]
+        )
+
+    for k in range(fan):
+        fetch(0, 0, k).start()
 
     def one_batch(batch, slot):
         def tile(j, carry):
             t = batch * BATCH + j
-            live = lax.rem(t, 3) < counts[lax.div(t, 3), 0, 0]
-            at = pl.multiple_of(lax.rem(t, 3) * rows, rows)
-
-            @pl.when(live)
+            m, place = lax.div(t, 3), lax.rem(t, 3)
+            live = place < counts[m, 0, 0]
+            at = pl.ds(pl.multiple_of(jnp.maximum(place - 1, 0) * rows, rows), rows)
+
+            @pl.when(live & (place > 0))
             def _():
-                def group(g, inner):
-                    for u in range(UNROLL):
-                        r = g * UNROLL + u
-
-                        def node(k):
-                            return nodes[pl.ds(ids[slot][k][j, r], 1), :]
-
-                        total = node(1)
-                        for k in range(2, fan):
-                            total = total + node(k)
-                        sums[pl.ds(r, 1), :] = jnp.where(lane_row < block, node(0), total)
-                    return inner
-
-                lax.fori_loop(0, rows // UNROLL, group, 0)
-                held = sums[...]
-                held = jnp.where(lane < block, held, held / (fan - 1.0))
-                turned = held.T.astype(out.dtype)
-                out[lax.div(t, 3), 0, :, pl.ds(at, rows)] = turned[:block]
-                out[lax.div(t, 3), 1, :, pl.ds(at, rows)] = turned[block : 2 * block]
+                turned = tile_sums(nodes, sums, flat[slot], rows, block, j * rows)
+                out[m, 0, :, at] = turned[:block]
+                out[m, 1, :, at] = turned[block : 2 * block]
 
             @pl.when(jnp.logical_not(live))
             def _():
-                out[lax.div(t, 3), :, :, pl.ds(at, rows)] = jnp.zeros((2, block, rows), out.dtype)
+                out[m, :, :, at] = jnp.zeros((2, block, rows), out.dtype)
 
             return carry
 
@@ -109,85 +233,38 @@
     lax.fori_loop(0, batches // 2, pair, 0)
 
 
-def gather(counts, ids, table):
+def gather(counts, ids, nodes, block):
     fan, tiles, rows = ids.shape
-    block, count = table.shape
-    owned = 3
+    vmem = pl.BlockSpec(memory_space=pltpu.VMEM)
     return pl.pallas_call(
         gather_kernel,
-        in_specs=[
-            pl.BlockSpec(memory_space=pltpu.SMEM),
-            pl.BlockSpec(memory_space=pl.ANY),
-            pl.BlockSpec(memory_space=pl.ANY),
-        ],
-        out_specs=pl.BlockSpec(memory_space=pltpu.VMEM),
-        scratch_shapes=[
-            pltpu.VMEM((count, 128), jnp.float32),
-            pltpu.VMEM((rows, 128), jnp.float32),
-            pltpu.VMEM((block, count), table.dtype),
-            pltpu.SemaphoreType.DMA((LOADS,)),
-        ]
+        in_specs=[pl.BlockSpec(memory_space=pltpu.SMEM), pl.BlockSpec(memory_space=pl.ANY), vmem],
+        out_specs=vmem,
+        scratch_shapes=[pltpu.VMEM((rows, 128), jnp.float32)]
         + [pltpu.SMEM((BATCH, rows), jnp.int32)] * (2 * fan)
         + [pltpu.SemaphoreType.DMA((2, fan))],
-        out_shape=jax.ShapeDtypeStruct((tiles // owned, 2, block, owned * rows), jnp.bfloat16),
-        compiler_params=pltpu.CompilerParams(vmem_limit_bytes=56 << 20),
+        out_shape=jax.ShapeDtypeStruct((tiles // 3, 2, block, 2 * rows), jnp.bfloat16),
+        compiler_params=pltpu.CompilerParams(vmem_limit_bytes=16 << 20),
         cost_estimate=pl.CostEstimate(
-            flops=120_000_000_000, bytes_accessed=300_000_000, transcendentals=0
+            flops=60_000_000_000, bytes_accessed=150_000_000, transcendentals=0
         ),
-    )(counts, ids, table)
-
-
-def count_kernel(count, out, got, send_sem, recv_sem):
-    f = lax.axis_index("feat")
-    peers = out.shape[0]
-    barrier = pltpu.get_barrier_semaphore()
-    for i in range(1, peers):
-        pl.semaphore_signal(
-            barrier, inc=1, device_id={"feat": lax.rem(f + i, peers)}, device_id_type=MESH
-        )
-    got[f] = jnp.zeros(got.shape[1:], jnp.int32) + count[0]
-    pl.semaphore_wait(barrier, peers - 1)
-    copies = []
-    for i in range(1, peers):
-        copy = pltpu.make_async_remote_copy(
-            src_ref=got.at[f],
-            dst_ref=got.at[f],
-            send_sem=send_sem.at[i],
-            recv_sem=recv_sem.at[i],
-            device_id={"feat": lax.rem(f + i, peers)},
-            device_id_type=MESH,
-        )
+    )(counts, ids, nodes)
+
+
+def finish_kernel(a, b, c, out_a, out_b, out_c, held_a, held_b, held_c, sem):
+    moves = []
+    for q in range(4):
+        at = pl.ds(q * (a.shape[0] // 4), a.shape[0] // 4)
+        moves.append((a.at[at], held_a.at[at], out_a.at[at]))
+    moves += [(b, held_b, out_b), (c, held_c, out_c)]
+    ins = [pltpu.make_async_copy(x, h, sem.at[0, i]) for i, (x, h, _) in enumerate(moves)]
+    outs = [pltpu.make_async_copy(h, o, sem.at[1, i]) for i, (_, h, o) in enumerate(moves)]
+    for copy in ins:
         copy.start()
-        copies.append(copy)
-    for copy in copies:
-        copy.wait()
-    out[...] = got[...]
-
-
-def exchange_counts(count):
-    peers = 16
-    return pl.pallas_call(
-        count_kernel,
-        in_specs=[pl.BlockSpec(memory_space=pltpu.SMEM)],
-        out_specs=pl.BlockSpec(memory_space=pltpu.VMEM),
-        out_shape=jax.ShapeDtypeStruct((peers, 1, 128), jnp.int32),
-        scratch_shapes=[
-            pltpu.VMEM((peers, 1, 128), jnp.int32),
-            pltpu.SemaphoreType.DMA((peers,)),
-            pltpu.SemaphoreType.DMA((peers,)),
-        ],
-        compiler_params=pltpu.CompilerParams(collective_id=1, has_side_effects=True),
-    )(count)
-
-
-def finish_kernel(a, b, c, out_a, out_b, out_c, sem):
-    copies = [
-        pltpu.make_async_copy(x, y, sem.at[i])
-        for i, (x, y) in enumerate(((a, out_a), (b, out_b), (c, out_c)))
-    ]
-    for copy in copies:
-        copy.start()
-    for copy in copies:
+    for arrived, leaving in zip(ins, outs):
+        arrived.wait()
+        leaving.start()
+    for copy in outs:
         copy.wait()
 
 
@@ -197,13 +274,14 @@
         in_specs=[pl.BlockSpec(memory_space=pl.ANY)] * 3,
         out_specs=[pl.BlockSpec(memory_space=pl.ANY)] * 3,
         out_shape=[jax.ShapeDtypeStruct(x.shape, x.dtype) for x in arrays],
-        scratch_shapes=[pltpu.SemaphoreType.DMA((3,))],
+        scratch_shapes=[pltpu.VMEM(x.shape, x.dtype) for x in arrays]
+        + [pltpu.SemaphoreType.DMA((2, 6))],
         compiler_params=pltpu.CompilerParams(vmem_limit_bytes=56 << 20),
     )(*arrays)
 
 
 def layer_kernel(
-    live_count, x, w_self, w_neigh, bias, cot, act, out_self, out_neigh,
+    live_count, first, x, w_self, w_neigh, bias, cot, act, out_self, out_neigh,
     w, mine, turned, delta, other, pair_in, part_a, relay_a, in_a, part_b, relay_b, in_b,
     y_out, y_in, half, half_in, x_send, x_recv, p_send, p_recv, r_send, r_recv, y_send, y_recv, h_send, h_recv, local_sem, w_sem,
 ):
@@ -236,14 +314,18 @@
         pl.semaphore_signal(barrier, inc=1, device_id={"dp": at * 2 + core}, device_id_type=MESH)
     pl.semaphore_wait(barrier, 18)
 
+    tile_rows = rows // 3
+    early = pltpu.make_async_copy(first, mine.at[:, :, pl.ds(0, tile_rows)], local_sem.at[0])
+    early.start()
     my_rows = pl.ds(pl.multiple_of(f * block, block), block)
-    own = pltpu.make_async_copy(x.at[f], mine.at[:, my_rows], local_sem)
+    later = pl.ds(tile_rows, rows - tile_rows)
+    own = pltpu.make_async_copy(x.at[f], mine.at[:, my_rows, later], local_sem.at[1])
     own.start()
     sends = []
     for i, j in others:
         copy = pltpu.make_async_remote_copy(
             src_ref=x.at[feat_peer(i, j)],
-            dst_ref=mine.at[:, my_rows],
+            dst_ref=mine.at[:, my_rows, later],
             send_sem=x_send.at[i * 4 + j],
             recv_sem=x_recv.at[i * 4 + j],
             device_id={"feat": feat_peer(i, j)},
@@ -251,36 +333,43 @@
         )
         copy.start()
         sends.append(copy)
+
+    def turn(lo, size):
+        def step(i, carry):
+            at = pl.multiple_of(i * 128, 128)
+            for p in range(2):
+                to = pl.multiple_of(p * half_wide + i * 128, 128)
+                turned[lo : lo + size, pl.ds(to, 128)] = mine[p, pl.ds(at, 128), lo : lo + size].T
+            return carry
+
+        lax.fori_loop(0, half_wide // 128, step, 0)
+
+    def forward(lo, size):
+        tile_of = lax.div(lax.broadcasted_iota(jnp.int32, (size, 256), 0) + lo, tile_rows)
+        live = tile_of < live_count[0]
+
+        def step(n, carry):
+            at = pl.ds(pl.multiple_of(n * 256, 256), 256)
+            pre = jnp.dot(turned[lo : lo + size], w[:, at], preferred_element_type=jnp.float32)
+            pre = pre + bias[:, at]
+            on = live & (pre > 0)
+            act[lo : lo + size, at] = jnp.where(on, pre, 0.0).astype(act.dtype)
+            c = cot[lo : lo + size, at].astype(jnp.float32)
+            delta[lo : lo + size, at] = jnp.where(on, c, 0.0).astype(delta.dtype)
+            return carry
+
+        lax.fori_loop(0, hidden // 256, step, 0)
+
+    early.wait()
+    turn(0, tile_rows)
+    for copy in weights:
+        copy.wait()
+    forward(0, tile_rows)
     own.wait()
     for copy in sends:
         copy.wait()
-
-    def turn(i, carry):
-        at = pl.multiple_of(i * 128, 128)
-        for p in range(2):
-            to = pl.multiple_of(p * half_wide + i * 128, 128)
-            turned[:, pl.ds(to, 128)] = mine[p, pl.ds(at, 128), :].T
-        return carry
-
-    lax.fori_loop(0, half_wide // 128, turn, 0)
-    for copy in weights:
-        copy.wait()
-
-    tile_rows = rows // 3
-    tile_of = lax.div(lax.broadcasted_iota(jnp.int32, (rows, 256), 0), tile_rows)
-    live = tile_of < live_count[0]
-
-    def forward(n, carry):
-        at = pl.multiple_of(n * 256, 256)
-        pre = jnp.dot(turned[...], w[:, pl.ds(at, 256)], preferred_element_type=jnp.float32)
-        pre = pre + bias[:, pl.ds(at, 256)]
-        on = live & (pre > 0)
-        act[:, pl.ds(at, 256)] = jnp.where(on, pre, 0.0).astype(act.dtype)
-        c = cot[:, pl.ds(at, 256)].astype(jnp.float32)
-        delta[:, pl.ds(at, 256)] = jnp.where(on, c, 0.0).astype(delta.dtype)
-        return carry
-
-    lax.fori_loop(0, hidden // 256, forward, 0)
+    turn(tile_rows, rows - tile_rows)
+    forward(tile_rows, rows - tile_rows)
 
     quarter = cols // 2
 
@@ -411,8 +500,8 @@
         copy.wait_send()
 
 
-def layer(count, x, w_self, w_neigh, bias, cot):
-    peers, _, block, rows = x.shape
+def layer(count, first, x, w_self, w_neigh, bias, cot):
+    block, rows = x.shape[2], cot.shape[0]
     half_wide, hidden = w_self.shape
     quarter = hidden // 4
     bf16, f32 = jnp.bfloat16, jnp.float32
@@ -421,7 +510,7 @@
     dma = pltpu.SemaphoreType.DMA
     return pl.pallas_call(
         layer_kernel,
-        in_specs=[pl.BlockSpec(memory_space=pltpu.SMEM), hbm, hbm, hbm, vmem, vmem],
+        in_specs=[pl.BlockSpec(memory_space=pltpu.SMEM), hbm, hbm, hbm, hbm, vmem, vmem],
         out_specs=[vmem, vmem, vmem],
         out_shape=[
             jax.ShapeDtypeStruct((rows, hidden), bf16),
@@ -446,7 +535,7 @@
             pltpu.VMEM((2, 2, block, quarter), f32),
             pltpu.VMEM((2, 2, block, quarter), f32),
             dma((16,)), dma((16,)), dma((4,)), dma((4,)), dma((2, 2, 6)), dma((2, 2, 6)),
-            dma((2, 2)), dma((2, 2)), dma((2,)), dma((2,)), dma, dma((2,)),
+            dma((2, 2)), dma((2, 2)), dma((2,)), dma((2,)), dma((2,)), dma((2,)),
         ],
         compiler_params=pltpu.CompilerParams(
             collective_id=0, has_side_effects=True, vmem_limit_bytes=56 << 20
@@ -454,16 +543,19 @@
         cost_estimate=pl.CostEstimate(
             flops=2_500_000_000, bytes_accessed=10_000_000, transcendentals=0
         ),
-    )(count, x, w_self, w_neigh, bias, cot)
+    )(count, first, x, w_self, w_neigh, bias, cot)
 
 
 def local(node_table, neighbor_ids, tile_counts, w_self, w_neigh, bias, cotangent):
     owned, rows, hidden = cotangent.shape
     w_self_all = lax.all_gather(w_self, "feat", axis=0, tiled=True)
     w_neigh_all = lax.all_gather(w_neigh, "feat", axis=0, tiled=True)
-    x = gather(exchange_counts(tile_counts), neighbor_ids.transpose(1, 0, 2), node_table)
+    ids = neighbor_ids.transpose(1, 0, 2)
+    nodes, counts, first = first_tiles(tile_counts, ids, node_table)
+    x = gather(counts, ids, nodes, node_table.shape[0])
     act, grad_self, grad_neigh = layer(
         tile_counts,
+        first,
         x,
         w_self_all,
         w_neigh_all,

time: 220 us -> 176 us (0.80)
  Pallas kernels: 202 us -> 156 us
  local copies, waits for them, and re-layouts: 0 us -> 2.68 us
    pallas_call x1, Pallas kernels: 89.7 us -> 49.1 us  [gather(): pl.pallas_call(gather_kernel, in_specs=[pl.BlockSpec(memory_space=pltpu.S...]
    pallas_call x1, Pallas kernels: 10.9 us -> 47.9 us  [first_tiles(): pl.pallas_call(first_kernel, in_specs=[pl.BlockSpec(memory_space=pltpu.SM...]
    pallas_call x1, Pallas kernels: 36.9 us -> 2.13 us  [finish(): pl.pallas_call(finish_kernel, in_specs=[pl.BlockSpec(memory_space=pl.ANY)...]
    pallas_call x1, Pallas kernels: 64.3 us -> 56.5 us  [layer(): pl.pallas_call(layer_kernel, in_specs=[pl.BlockSpec(memory_space=pltpu.SM...]
    unnamed x0 -> x6, local copies, waits for them, and re-layouts: none -> 2.68 us
  transfers between devices with their start and end apart: 2 -> 2, of which waited for: 0 -> 0; matrix products, arithmetic and copies ran while one was open for 0% -> 0% of each run, Pallas kernels for 46% -> 56%
where the time goes in v3:
time: 176 us; the launch traced here: 175 us
  Pallas kernels  156 us (89%)
  between operations  14.7 us (8%)
  local copies, waits for them, and re-layouts  2.68 us (2%)
    pallas_call x1, Pallas kernels, layer(): pl.pallas_call(layer_kernel, in_specs=[pl.BlockSpec(memory_space=pltpu.SM...  56.5 us
    pallas_call x1, Pallas kernels, gather(): pl.pallas_call(gather_kernel, in_specs=[pl.BlockSpec(memory_space=pltpu.S...  49.1 us
    pallas_call x1, Pallas kernels, first_tiles(): pl.pallas_call(first_kernel, in_specs=[pl.BlockSpec(memory_space=pltpu.SM...  47.9 us
  transfers between devices with their start and end apart: 2, of which 0 were waited for; matrix products, arithmetic and copies ran while one was open for 0% of the time, Pallas kernels for 56%

profile of v3, /device:TPU:1, one launch (start us, length us, event | category | flops | bytes accessed | tf_op | source)
XLA Modules:
  0.0 174.6 jit_solution(16393511063049691625)
XLA Ops:
  7.2 0.0 all-gather.3.cloned.1.call-start
  7.2 0.7 all-gather.3.cloned.1.call-update
  7.9 0.0 all-gather.5.cloned.1.call-start
  7.9 0.7 all-gather.5.cloned.1.call-update
  9.3 0.0 copy-start
  9.3 1.1 copy-done
  10.4 47.9 %shard_map.94 = (f32[65536,128]{1,0:T(8,128)S(1)}, s32[16,1,128]{2,1,0:T(1,128)S(1)}, bf16[2,768,128]{2,1,0:T(8,128)(2,1)S(1)}) custom-call(s32[1]{0:T(128)S(6)} %copy.10.count.live_count, s32[26,48,128]{2,1,0:T(8,128)S(1)} %bitcast.4, bf16[48,65536]{1,0:T(8,128)(2,1)} %table_hbm.1), custom_call_target="tpu_custom_call" | custom-call | flops 60000002048 | bytes 150000000 | tf_op jit(solution)/shard_map/pallas_call | solution.py:150
  58.3 0.0 copy-start.2
  58.3 0.7 copy-done.2
  59.1 49.1 %shard_map.95.x = bf16[16,2,48,256]{3,2,1,0:T(8,128)(2,1)S(1)} custom-call(s32[16,1,128]{2,1,0:T(1,128)S(1)} %get-tuple-element.13.counts, s32[26,48,128]{2,1,0:T(8,128)S(1)} %bitcast.5, f32[65536,128]{1,0:T(8,128)S(1)} %get-tuple-element.14.nodes), custom_call_target="tpu_custom_call" | custom-call | flops 60000002048 | bytes 150000000 | tf_op jit(solution)/shard_map/pallas_call | solution.py:239
  108.1 0.0 copy-start.1
  108.2 0.9 copy-done.1
  109.0 0.0 all-gather.3.cloned.1.call-done.w_self
  109.0 0.0 all-gather.5.cloned.1.call-done.w_neigh
  109.0 56.5 %shard_map.96 = (bf16[384,1024]{1,0:T(8,128)(2,1)}, f32[48,1024]{1,0:T(8,128)}, f32[48,1024]{1,0:T(8,128)}) custom-call(s32[1]{0:T(128)S(6)} %copy.10.count.live_count, bf16[2,768,128]{2,1,0:T(8,128)(2,1)} %copy-done.2, bf16[16,2,48,256]{3,2,1,0:T(8,128)(2,1)} %copy-done.1, bf16[768,1024]{1,0:T(8,128)(2,1)} %all-gather.3.cloned.1.call-done.w_self, ...), custom_call_target="tpu_custom_call" | custom-call | flops 2500000000 | bytes 10000000 | tf_op jit(solution)/shard_map/pallas_call | solution.py:511
  165.6 2.1 %shard_map.97 = (bf16[384,1024]{1,0:T(8,128)(2,1)}, f32[48,1024]{1,0:T(8,128)}, f32[48,1024]{1,0:T(8,128)}) custom-call(bf16[384,1024]{1,0:T(8,128)(2,1)} %get-tuple-element.15.a, f32[48,1024]{1,0:T(8,128)} %get-tuple-element.16.b, f32[48,1024]{1,0:T(8,128)} %get-tuple-element.17.c), custom_call_target="tpu_custom_call" | custom-call | tf_op jit(solution)/shard_map/pallas_call | solution.py:272
Async XLA Ops:
  7.2 101.9 %all-gather.3.cloned.1.call-start = ((), (), s32[]{:S(2)}) async-start(), calls=%async_computation | async-start | bytes 1671168 | tf_op jit(solution)/shard_map/all_gather | solution.py:551
  7.9 101.1 %all-gather.5.cloned.1.call-start = ((), (), s32[]{:S(2)}) async-start(), calls=%async_computation.1 | async-start | bytes 1671168 | tf_op jit(solution)/shard_map/all_gather | solution.py:552
  9.3 1.1 copy-start
  58.3 0.7 copy-start.2
  108.1 0.9 copy-start.1
Sparse Core Ops, SparseCore 0:
  10.1 46.5 all-gather.2
  58.9 44.5 all-gather.4

commit v4 on v3

--- a/solution.py
+++ b/solution.py
@@ -6,10 +6,11 @@
 from jax.sharding import PartitionSpec as P
 
 MESH = pl.DeviceIdType.MESH
-UNROLL = 16
+UNROLL = 32
 BATCH = 8
 CHUNK = 2048
 LOADS = 8
+DIRECT = (False, True)
 
 
 def tile_sums(nodes, sums, ids, rows, block, base):
@@ -36,11 +37,13 @@
 
 
 def first_kernel(
-    count, ids_hbm, table_hbm, nodes, counts, first, table, sums, sent, landed, got, *rest
+    count, ids_hbm, table_hbm, w_self, w_neigh, nodes, counts, first, weights,
+    table, sums, sent, landed, got, w_got, *rest
 ):
     fan, _, rows = ids_hbm.shape
     ids = (rest[:fan], rest[fan : 2 * fan])
-    ids_sem, load_sem, c_send, c_recv, x_send, x_recv = rest[2 * fan :]
+    ids_sem, load_sem, c_send, c_recv, x_send, x_recv, w_send, w_recv, w_sem = rest[2 * fan :]
+    core = lax.rem(lax.axis_index("dp"), 2)
     block, width = table_hbm.shape
     peers = got.shape[0]
     f = lax.axis_index("feat")
@@ -91,6 +94,12 @@
 
     my_rows = pl.ds(pl.multiple_of(f * block, block), block)
 
+    def weight_copy(source, i):
+        return pltpu.make_async_remote_copy(
+            src_ref=source, dst_ref=w_got.at[my_rows], send_sem=w_send.at[i], recv_sem=w_recv.at[i],
+            device_id={"feat": peer(i)}, device_id_type=MESH,
+        )
+
     def tile_copy(i):
         return pltpu.make_async_remote_copy(
             src_ref=sent.at[peer(i)], dst_ref=landed.at[:, my_rows],
@@ -100,6 +109,15 @@
 
     for i in range(1, peers):
         count_copy(i).start()
+    for which, source in enumerate((w_self, w_neigh)):
+
+        @pl.when(core == which)
+        def _():
+            keep = pltpu.make_async_copy(source, w_got.at[my_rows], w_sem)
+            keep.start()
+            for i in range(1, peers):
+                weight_copy(source, i).start()
+            keep.wait()
 
     def pair(p, carry):
         for slot in range(2):
@@ -133,28 +151,34 @@
     def settle(i, carry):
         count_copy(i).wait()
         tile_copy(i).wait()
+        weight_copy(w_self, i).wait()
         return carry
 
     lax.fori_loop(1, peers, settle, 0)
+    keep = pltpu.make_async_copy(w_got, weights, w_sem)
+    keep.start()
+    keep.wait()
     counts[...] = got[...]
     first[...] = landed[...]
 
 
-def first_tiles(count, ids, table):
+def first_tiles(count, ids, table, w_self, w_neigh):
     fan, tiles, rows = ids.shape
     block, width = table.shape
+    hidden = w_self.shape[1]
     peers = tiles // 3
     dma = pltpu.SemaphoreType.DMA
     hbm = pl.BlockSpec(memory_space=pl.ANY)
     vmem = pl.BlockSpec(memory_space=pltpu.VMEM)
-    nodes, counts, first = pl.pallas_call(
+    nodes, counts, first, weights = pl.pallas_call(
         first_kernel,
-        in_specs=[pl.BlockSpec(memory_space=pltpu.SMEM), hbm, hbm],
-        out_specs=[vmem, vmem, vmem],
+        in_specs=[pl.BlockSpec(memory_space=pltpu.SMEM), hbm, hbm, hbm, hbm],
+        out_specs=[vmem, vmem, vmem, hbm],
         out_shape=[
             pltpu.VMEM((width, 128), jnp.float32),
             jax.ShapeDtypeStruct((peers, 1, 128), jnp.int32),
             jax.ShapeDtypeStruct((2, peers * block, rows), jnp.bfloat16),
+            jax.ShapeDtypeStruct((peers * block, hidden), w_self.dtype),
         ],
         scratch_shapes=[
             pltpu.VMEM((block, width), table.dtype),
@@ -162,17 +186,20 @@
             pltpu.VMEM((peers, 2, block, rows), jnp.bfloat16),
             pltpu.VMEM((2, peers * block, rows), jnp.bfloat16),
             pltpu.VMEM((peers, 1, 128), jnp.int32),
+            pltpu.VMEM((peers * block, hidden), w_self.dtype),
         ]
         + [pltpu.SMEM((rows,), jnp.int32)] * (2 * fan)
-        + [dma((2, fan)), dma((LOADS,)), dma((peers,)), dma((peers,)), dma((peers,)), dma((peers,))],
+        + [dma((2, fan)), dma((LOADS,))]
+        + [dma((peers,))] * 6
+        + [dma],
         compiler_params=pltpu.CompilerParams(
-            collective_id=1, has_side_effects=True, vmem_limit_bytes=16 << 20
+            collective_id=1, has_side_effects=True, vmem_limit_bytes=28 << 20
         ),
         cost_estimate=pl.CostEstimate(
             flops=60_000_000_000, bytes_accessed=150_000_000, transcendentals=0
         ),
-    )(count, ids, table)
-    return pltpu.with_memory_space_constraint(nodes, pltpu.VMEM), counts, first
+    )(count, ids, table, w_self, w_neigh)
+    return pltpu.with_memory_space_constraint(nodes, pltpu.VMEM), counts, first, weights
 
 
 def gather_kernel(counts, ids_hbm, nodes, out, sums, *rest):
@@ -244,7 +271,7 @@
         + [pltpu.SMEM((BATCH, rows), jnp.int32)] * (2 * fan)
         + [pltpu.SemaphoreType.DMA((2, fan))],
         out_shape=jax.ShapeDtypeStruct((tiles // 3, 2, block, 2 * rows), jnp.bfloat16),
-        compiler_params=pltpu.CompilerParams(vmem_limit_bytes=16 << 20),
+        compiler_params=pltpu.CompilerParams(vmem_limit_bytes=28 << 20),
         cost_estimate=pl.CostEstimate(
             flops=60_000_000_000, bytes_accessed=150_000_000, transcendentals=0
         ),
@@ -281,9 +308,9 @@
 
 
 def layer_kernel(
-    live_count, first, x, w_self, w_neigh, bias, cot, act, out_self, out_neigh,
+    live_count, first, x, w_half, bias, cot, act, out_self, out_neigh,
     w, mine, turned, delta, other, pair_in, part_a, relay_a, in_a, part_b, relay_b, in_b,
-    y_out, y_in, half, half_in, x_send, x_recv, p_send, p_recv, r_send, r_recv, y_send, y_recv, h_send, h_recv, local_sem, w_sem,
+    y_in, half, half_in, x_send, x_recv, p_send, p_recv, r_send, r_recv, y_send, y_recv, h_send, h_recv, local_sem, w_sem,
 ):
     f, d = lax.axis_index("feat"), lax.axis_index("dp")
     z, xx = lax.div(f, 4), lax.rem(f, 4)
@@ -297,23 +324,28 @@
     def feat_peer(i, j):
         return lax.rem(z + i, 4) * 4 + lax.rem(xx + j, 4)
 
+    def y_peer(i):
+        return {"dp": lax.rem(y + i, 4) * 2 + core}
+
     others = [(i, j) for i in range(4) for j in range(4) if (i, j) != (0, 0)]
 
-    weights = [
-        pltpu.make_async_copy(part, w.at[pl.ds(p * half_wide, half_wide)], w_sem.at[p])
-        for p, part in enumerate((w_self, w_neigh))
-    ]
-    for copy in weights:
-        copy.start()
+    w_rows = pl.ds(pl.multiple_of(core * half_wide, half_wide), half_wide)
+    w_own = pltpu.make_async_copy(w_half, w.at[w_rows], w_sem.at[0])
+    w_own.start()
 
     barrier = pltpu.get_barrier_semaphore()
     for i, j in others:
         pl.semaphore_signal(barrier, inc=1, device_id={"feat": feat_peer(i, j)}, device_id_type=MESH)
     pl.semaphore_signal(barrier, inc=1, device_id=partner, device_id_type=MESH)
-    for at in (y + 1 - 2 * lax.rem(y, 2), 3 - y):
-        pl.semaphore_signal(barrier, inc=1, device_id={"dp": at * 2 + core}, device_id_type=MESH)
-    pl.semaphore_wait(barrier, 18)
-
+    for i in range(1, 4):
+        pl.semaphore_signal(barrier, inc=1, device_id=y_peer(i), device_id_type=MESH)
+    pl.semaphore_wait(barrier, 19)
+
+    w_other = pltpu.make_async_remote_copy(
+        src_ref=w_half, dst_ref=w.at[w_rows], send_sem=w_sem.at[1], recv_sem=w_sem.at[2],
+        device_id=partner, device_id_type=MESH,
+    )
+    w_other.start()
     tile_rows = rows // 3
     early = pltpu.make_async_copy(first, mine.at[:, :, pl.ds(0, tile_rows)], local_sem.at[0])
     early.start()
@@ -362,8 +394,8 @@
 
     early.wait()
     turn(0, tile_rows)
-    for copy in weights:
-        copy.wait()
+    w_own.wait()
+    w_other.wait()
     forward(0, tile_rows)
     own.wait()
     for copy in sends:
@@ -418,7 +450,24 @@
                 src, dst, r_send.at[phase, h, m], r_recv.at[phase, h, m], neighbour(h, phase, step)
             )
 
+    def direct(h, phase, p):
+        part, _, arrived = (buffer.at[h] for buffer in phases[phase])
+        for s in (2, 1, 3):
+            m = (s - 1) * 2 + p
+            started[h, phase, m] = remote(
+                part.at[lax.rem(place(h, phase) + s, 4), p], arrived.at[s - 1, p],
+                r_send.at[phase, h, m], r_recv.at[phase, h, m], neighbour(h, phase, s),
+            )
+
+    def send_part(h, phase, p):
+        if DIRECT[phase]:
+            direct(h, phase, p)
+        else:
+            ring(h, phase, (0, 3) if p == 0 else (1, 2))
+
     def pass_on(h, phase):
+        if DIRECT[phase]:
+            return
         part, relay, _ = (buffer.at[h] for buffer in phases[phase])
         pos = place(h, phase)
         for way, step in ((0, 1), (1, 3)):
@@ -431,13 +480,13 @@
 
     def gathered(h, phase, p):
         part, _, arrived = (buffer.at[h] for buffer in phases[phase])
-        for m in ((4, 3), (2, 5))[p]:
+        from_peers = (p, 2 + p, 4 + p) if DIRECT[phase] else ((4, 3), (2, 5))[p]
+        total = part[place(h, phase), p].astype(jnp.float32)
+        for m in from_peers:
             started[h, phase, m].wait_recv()
-        return (
-            part[place(h, phase), p].astype(jnp.float32)
-            + arrived[0, p].astype(jnp.float32)
-            + arrived[1, p].astype(jnp.float32)
-        )
+        for i in range(len(from_peers)):
+            total = total + arrived[i, p].astype(jnp.float32)
+        return total
 
     order = ((0, 0), (0, 1), (1, 0), (1, 1))
     pairs = []
@@ -455,7 +504,7 @@
                     part_a[h, j, p, i] = rows_ij
                 else:
                     part_a[h, i, p, j] = rows_ij
-        ring(h, 0, (0, 3) if p == 0 else (1, 2))
+        send_part(h, 0, p)
         if q >= 2:
             pass_on(q - 2, 0)
     for h in range(2):
@@ -463,32 +512,26 @@
             reduced = gathered(h, 0, p).astype(part_b.dtype)
             for i in range(4):
                 part_b[h, i, p] = reduced[i]
-            ring(h, 1, (0, 3) if p == 0 else (1, 2))
+            send_part(h, 1, p)
     for h in range(2):
         pass_on(h, 1)
-
-    def y_peer_of(h, stage):
-        at = y + 1 - 2 * lax.rem(y, 2) if (h + stage) % 2 == 0 else 3 - y
-        return {"dp": at * 2 + core}
 
     across = {}
     for h in range(2):
         for p in range(2):
-            y_out[h, 0, p] = gathered(h, 1, p).astype(y_out.dtype)
-        across[h, 0] = remote(
-            y_out.at[h, 0], y_in.at[h, 0], y_send.at[h, 0], y_recv.at[h, 0], y_peer_of(h, 0)
-        )
-    for h in range(2):
-        across[h, 0].wait_recv()
-        both = y_out[h, 0].astype(jnp.float32) + y_in[h, 0].astype(jnp.float32)
-        y_out[h, 1] = both.astype(y_out.dtype)
-        across[h, 1] = remote(
-            y_out.at[h, 1], y_in.at[h, 1], y_send.at[h, 1], y_recv.at[h, 1], y_peer_of(h, 1)
-        )
+            y_in[h, y, p] = gathered(h, 1, p).astype(y_in.dtype)
+        for i in (2, 1, 3):
+            across[h, i] = remote(
+                y_in.at[h, y], y_in.at[h, y], y_send.at[h, i], y_recv.at[h, i], y_peer(i)
+            )
     last = []
     for h in range(2):
-        across[h, 1].wait_recv()
-        half[h] = y_out[h, 1].astype(jnp.float32) + y_in[h, 1].astype(jnp.float32)
+        for i in range(1, 4):
+            across[h, i].wait_recv()
+        total = y_in[h, 0].astype(jnp.float32)
+        for i in range(1, 4):
+            total = total + y_in[h, i].astype(jnp.float32)
+        half[h] = total
         last.append(remote(half.at[h], half_in.at[h], h_send.at[h], h_recv.at[h], partner))
         out_self[:, ours(h)] = half[h, 0]
         out_neigh[:, ours(h)] = half[h, 1]
@@ -500,9 +543,9 @@
         copy.wait_send()
 
 
-def layer(count, first, x, w_self, w_neigh, bias, cot):
+def layer(count, first, x, w_half, bias, cot):
     block, rows = x.shape[2], cot.shape[0]
-    half_wide, hidden = w_self.shape
+    half_wide, hidden = w_half.shape
     quarter = hidden // 4
     bf16, f32 = jnp.bfloat16, jnp.float32
     vmem = pl.BlockSpec(memory_space=pltpu.VMEM)
@@ -510,7 +553,7 @@
     dma = pltpu.SemaphoreType.DMA
     return pl.pallas_call(
         layer_kernel,
-        in_specs=[pl.BlockSpec(memory_space=pltpu.SMEM), hbm, hbm, hbm, hbm, vmem, vmem],
+        in_specs=[pl.BlockSpec(memory_space=pltpu.SMEM), hbm, hbm, hbm, vmem, vmem],
         out_specs=[vmem, vmem, vmem],
         out_shape=[
             jax.ShapeDtypeStruct((rows, hidden), bf16),
@@ -526,16 +569,15 @@
             pltpu.VMEM((4, half_wide, quarter), bf16),
             pltpu.VMEM((2, 4, 2, 4, block, quarter), bf16),
             pltpu.VMEM((2, 2, 4, block, quarter), bf16),
-            pltpu.VMEM((2, 2, 2, 4, block, quarter), bf16),
+            pltpu.VMEM((2, 3, 2, 4, block, quarter), bf16),
             pltpu.VMEM((2, 4, 2, block, quarter), bf16),
             pltpu.VMEM((2, 2, block, quarter), bf16),
-            pltpu.VMEM((2, 2, 2, block, quarter), bf16),
-            pltpu.VMEM((2, 2, 2, block, quarter), bf16),
-            pltpu.VMEM((2, 2, 2, block, quarter), bf16),
+            pltpu.VMEM((2, 3, 2, block, quarter), bf16),
+            pltpu.VMEM((2, 4, 2, block, quarter), bf16),
             pltpu.VMEM((2, 2, block, quarter), f32),
             pltpu.VMEM((2, 2, block, quarter), f32),
             dma((16,)), dma((16,)), dma((4,)), dma((4,)), dma((2, 2, 6)), dma((2, 2, 6)),
-            dma((2, 2)), dma((2, 2)), dma((2,)), dma((2,)), dma((2,)), dma((2,)),
+            dma((2, 4)), dma((2, 4)), dma((2,)), dma((2,)), dma((2,)), dma((3,)),
         ],
         compiler_params=pltpu.CompilerParams(
             collective_id=0, has_side_effects=True, vmem_limit_bytes=56 << 20
@@ -543,22 +585,19 @@
         cost_estimate=pl.CostEstimate(
             flops=2_500_000_000, bytes_accessed=10_000_000, transcendentals=0
         ),
-    )(count, first, x, w_self, w_neigh, bias, cot)
+    )(count, first, x, w_half, bias, cot)
 
 
 def local(node_table, neighbor_ids, tile_counts, w_self, w_neigh, bias, cotangent):
     owned, rows, hidden = cotangent.shape
-    w_self_all = lax.all_gather(w_self, "feat", axis=0, tiled=True)
-    w_neigh_all = lax.all_gather(w_neigh, "feat", axis=0, tiled=True)
     ids = neighbor_ids.transpose(1, 0, 2)
-    nodes, counts, first = first_tiles(tile_counts, ids, node_table)
+    nodes, counts, first, w_half = first_tiles(tile_counts, ids, node_table, w_self, w_neigh)
     x = gather(counts, ids, nodes, node_table.shape[0])
     act, grad_self, grad_neigh = layer(
         tile_counts,
         first,
         x,
-        w_self_all,
-        w_neigh_all,
+        w_half,
         bias.reshape(1, hidden),
         cotangent.reshape(owned * rows, hidden),
     )

time: 176 us -> 160 us (0.909)
  between operations: 14.7 us -> 1.3 us
  Pallas kernels: 156 us -> 159 us
  local copies, waits for them, and re-layouts: 2.68 us -> 0 us
    pallas_call x1, Pallas kernels: 56.5 us -> 61 us  [layer(): pl.pallas_call(layer_kernel, in_specs=[pl.BlockSpec(memory_space=pltpu.SM...]
    pallas_call x1, Pallas kernels: 49.1 us -> 44.9 us  [gather(): pl.pallas_call(gather_kernel, in_specs=[pl.BlockSpec(memory_space=pltpu.S...]
    unnamed x6 -> x0, local copies, waits for them, and re-layouts: 2.68 us -> none
    pallas_call x1, Pallas kernels: 47.9 us -> 50.6 us  [first_tiles(): pl.pallas_call(first_kernel, in_specs=[pl.BlockSpec(memory_space=pltpu.SM...]
  transfers between devices with their start and end apart: 2 -> 0, of which waited for: 0 -> 0; matrix products, arithmetic and copies ran while one was open for 0% -> 0% of each run, Pallas kernels for 56% -> 0%
where the time goes in v4:
time: 160 us
  Pallas kernels  159 us (99%)
    pallas_call x1, Pallas kernels, layer(): pl.pallas_call(layer_kernel, in_specs=[pl.BlockSpec(memory_space=pltpu.SM...  61 us
    pallas_call x1, Pallas kernels, first_tiles(): pl.pallas_call(first_kernel, in_specs=[pl.BlockSpec(memory_space=pltpu.SM...  50.6 us
    pallas_call x1, Pallas kernels, gather(): pl.pallas_call(gather_kernel, in_specs=[pl.BlockSpec(memory_space=pltpu.S...  44.9 us

profile of v4, /device:TPU:1, one launch (start us, length us, event | category | flops | bytes accessed | tf_op | source)
XLA Modules:
  0.0 159.9 jit_solution(13744771129719381681)
XLA Ops:
  1.3 50.6 %shard_map.94 = (f32[65536,128]{1,0:T(8,128)S(1)}, s32[16,1,128]{2,1,0:T(1,128)}, bf16[2,768,128]{2,1,0:T(8,128)(2,1)}, bf16[768,1024]{1,0:T(8,128)(2,1)}) custom-call(s32[1]{0:T(128)S(6)} %copy.10.count.live_count, s32[26,48,128]{2,1,0:T(8,128)} %bitcast.6, bf16[48,65536]{1,0:T(8,128)(2,1)} %table_hbm.1, bf16[48,1024]{1,0:T(8,128)(2,1)} %w_self.1, ...), custom_call_target="tpu_custom_call" | custom-call | flops 60000002048 | bytes 150000000 | tf_op jit(solution)/shard_map/pallas_call | solution.py:173
  51.8 44.9 %shard_map.95.x = bf16[16,2,48,256]{3,2,1,0:T(8,128)(2,1)} custom-call(s32[16,1,128]{2,1,0:T(1,128)} %get-tuple-element.14.counts, s32[26,48,128]{2,1,0:T(8,128)} %bitcast.7, f32[65536,128]{1,0:T(8,128)S(1)} %get-tuple-element.15.nodes), custom_call_target="tpu_custom_call" | custom-call | flops 60000002048 | bytes 150000000 | tf_op jit(solution)/shard_map/pallas_call | solution.py:266
  96.7 61.0 %shard_map.96 = (bf16[384,1024]{1,0:T(8,128)(2,1)}, f32[48,1024]{1,0:T(8,128)}, f32[48,1024]{1,0:T(8,128)}) custom-call(s32[1]{0:T(128)S(6)} %copy.10.count.live_count, bf16[2,768,128]{2,1,0:T(8,128)(2,1)} %get-tuple-element.13.first, bf16[16,2,48,256]{3,2,1,0:T(8,128)(2,1)} %shard_map.95.x, bf16[768,1024]{1,0:T(8,128)(2,1)} %get-tuple-element.16.w_half, ...), custom_call_target="tpu_custom_call" | custom-call | flops 2500000000 | bytes 10000000 | tf_op jit(solution)/shard_map/pallas_call | solution.py:554
  157.8 2.1 %shard_map.97 = (bf16[384,1024]{1,0:T(8,128)(2,1)}, f32[48,1024]{1,0:T(8,128)}, f32[48,1024]{1,0:T(8,128)}) custom-call(bf16[384,1024]{1,0:T(8,128)(2,1)} %get-tuple-element.17.a, f32[48,1024]{1,0:T(8,128)} %get-tuple-element.18.b, f32[48,1024]{1,0:T(8,128)} %get-tuple-element.19.c), custom_call_target="tpu_custom_call" | custom-call | tf_op jit(solution)/shard_map/pallas_call | solution.py:299

commit v5 on v4

--- a/solution.py
+++ b/solution.py
@@ -8,9 +8,8 @@
 MESH = pl.DeviceIdType.MESH
 UNROLL = 32
 BATCH = 8
-CHUNK = 2048
+CHUNK = 4096
 LOADS = 8
-DIRECT = (False, True)
 
 
 def tile_sums(nodes, sums, ids, rows, block, base):
@@ -83,7 +82,7 @@
         lax.fori_loop(0, piece // CHUNK, turn, 0)
         return carry
 
-    lax.fori_loop(0, LOADS, fill, 0)
+    lax.fori_loop(0, 2, fill, 0)
     pl.semaphore_wait(barrier, peers - 1)
 
     def count_copy(i):
@@ -118,6 +117,8 @@
             for i in range(1, peers):
                 weight_copy(source, i).start()
             keep.wait()
+
+    lax.fori_loop(2, LOADS, fill, 0)
 
     def pair(p, carry):
         for slot in range(2):
@@ -309,7 +310,7 @@
 
 def layer_kernel(
     live_count, first, x, w_half, bias, cot, act, out_self, out_neigh,
-    w, mine, turned, delta, other, pair_in, part_a, relay_a, in_a, part_b, relay_b, in_b,
+    w, mine, turned, delta, other, pair_in, part_a, in_a, part_b, in_b,
     y_in, half, half_in, x_send, x_recv, p_send, p_recv, r_send, r_recv, y_send, y_recv, h_send, h_recv, local_sem, w_sem,
 ):
     f, d = lax.axis_index("feat"), lax.axis_index("dp")
@@ -429,29 +430,11 @@
         at = lax.rem(place(h, phase) + 4 + s, 4)
         return {"feat": z * 4 + at if (h + phase) % 2 == 0 else at * 4 + xx}
 
-    phases = ((part_a, relay_a, in_a), (part_b, relay_b, in_b))
+    phases = ((part_a, in_a), (part_b, in_b))
     started = {}
 
-    def ring(h, phase, messages):
-        part, relay, arrived = (buffer.at[h] for buffer in phases[phase])
-        pos = place(h, phase)
-        far, after, before = (lax.rem(pos + s, 4) for s in (2, 1, 3))
-        plan = (
-            (1, part.at[far, 0], relay.at[0]),
-            (-1, part.at[far, 1], relay.at[1]),
-            (1, part.at[after, 1], arrived.at[0, 1]),
-            (-1, part.at[before, 0], arrived.at[1, 0]),
-            (1, part.at[after, 0], arrived.at[0, 0]),
-            (-1, part.at[before, 1], arrived.at[1, 1]),
-        )
-        for m in messages:
-            step, src, dst = plan[m]
-            started[h, phase, m] = remote(
-                src, dst, r_send.at[phase, h, m], r_recv.at[phase, h, m], neighbour(h, phase, step)
-            )
-
-    def direct(h, phase, p):
-        part, _, arrived = (buffer.at[h] for buffer in phases[phase])
+    def send_part(h, phase, p):
+        part, arrived = (buffer.at[h] for buffer in phases[phase])
         for s in (2, 1, 3):
             m = (s - 1) * 2 + p
             started[h, phase, m] = remote(
@@ -459,36 +442,15 @@
                 r_send.at[phase, h, m], r_recv.at[phase, h, m], neighbour(h, phase, s),
             )
 
-    def send_part(h, phase, p):
-        if DIRECT[phase]:
-            direct(h, phase, p)
-        else:
-            ring(h, phase, (0, 3) if p == 0 else (1, 2))
-
-    def pass_on(h, phase):
-        if DIRECT[phase]:
-            return
-        part, relay, _ = (buffer.at[h] for buffer in phases[phase])
-        pos = place(h, phase)
-        for way, step in ((0, 1), (1, 3)):
-            at = lax.rem(pos + step, 4)
-            started[h, phase, way].wait_recv()
-            part[at, way] = (
-                part[at, way].astype(jnp.float32) + relay[way].astype(jnp.float32)
-            ).astype(part.dtype)
-            ring(h, phase, (4 + way,))
-
     def gathered(h, phase, p):
-        part, _, arrived = (buffer.at[h] for buffer in phases[phase])
-        from_peers = (p, 2 + p, 4 + p) if DIRECT[phase] else ((4, 3), (2, 5))[p]
+        part, arrived = (buffer.at[h] for buffer in phases[phase])
         total = part[place(h, phase), p].astype(jnp.float32)
-        for m in from_peers:
-            started[h, phase, m].wait_recv()
-        for i in range(len(from_peers)):
+        for i in range(3):
+            started[h, phase, i * 2 + p].wait_recv()
             total = total + arrived[i, p].astype(jnp.float32)
         return total
 
-    order = ((0, 0), (0, 1), (1, 0), (1, 1))
+    order = ((0, 0), (1, 0), (0, 1), (1, 1))
     pairs = []
     for q, (h, p) in enumerate(order):
         other[q] = product(p, theirs(h)).astype(other.dtype)
@@ -505,17 +467,12 @@
                 else:
                     part_a[h, i, p, j] = rows_ij
         send_part(h, 0, p)
-        if q >= 2:
-            pass_on(q - 2, 0)
-    for h in range(2):
-        for p in range(2):
+    for p in range(2):
+        for h in range(2):
             reduced = gathered(h, 0, p).astype(part_b.dtype)
             for i in range(4):
                 part_b[h, i, p] = reduced[i]
             send_part(h, 1, p)
-    for h in range(2):
-        pass_on(h, 1)
-
     across = {}
     for h in range(2):
         for p in range(2):
@@ -568,10 +525,8 @@
             pltpu.VMEM((4, half_wide, quarter), bf16),
             pltpu.VMEM((4, half_wide, quarter), bf16),
             pltpu.VMEM((2, 4, 2, 4, block, quarter), bf16),
-            pltpu.VMEM((2, 2, 4, block, quarter), bf16),
             pltpu.VMEM((2, 3, 2, 4, block, quarter), bf16),
             pltpu.VMEM((2, 4, 2, block, quarter), bf16),
-            pltpu.VMEM((2, 2, block, quarter), bf16),
             pltpu.VMEM((2, 3, 2, block, quarter), bf16),
             pltpu.VMEM((2, 4, 2, block, quarter), bf16),
             pltpu.VMEM((2, 2, block, quarter), f32),

time: 160 us -> 153 us (0.956)
  Pallas kernels: 159 us -> 151 us
    pallas_call x1, Pallas kernels: 61 us -> 46.7 us  [layer(): pl.pallas_call(layer_kernel, in_specs=[pl.BlockSpec(memory_space=pltpu.SM...]
    pallas_call x1, Pallas kernels: 44.9 us -> 49 us  [gather(): pl.pallas_call(gather_kernel, in_specs=[pl.BlockSpec(memory_space=pltpu.S...]
    pallas_call x1, Pallas kernels: 50.6 us -> 53.1 us  [first_tiles(): pl.pallas_call(first_kernel, in_specs=[pl.BlockSpec(memory_space=pltpu.SM...]
where the time goes in v5:
time: 153 us; the launch traced here: 152 us
  Pallas kernels  151 us (99%)
    pallas_call x1, Pallas kernels, first_tiles(): pl.pallas_call(first_kernel, in_specs=[pl.BlockSpec(memory_space=pltpu.SM...  53.1 us
    pallas_call x1, Pallas kernels, gather(): pl.pallas_call(gather_kernel, in_specs=[pl.BlockSpec(memory_space=pltpu.S...  49 us
    pallas_call x1, Pallas kernels, layer(): pl.pallas_call(layer_kernel, in_specs=[pl.BlockSpec(memory_space=pltpu.SM...  46.7 us

profile of v5, /device:TPU:1, one launch (start us, length us, event | category | flops | bytes accessed | tf_op | source)
XLA Modules:
  0.0 152.3 jit_solution(13609716049434196144)
XLA Ops:
  1.3 53.1 %shard_map.94 = (f32[65536,128]{1,0:T(8,128)S(1)}, s32[16,1,128]{2,1,0:T(1,128)}, bf16[2,768,128]{2,1,0:T(8,128)(2,1)}, bf16[768,1024]{1,0:T(8,128)(2,1)}) custom-call(s32[1]{0:T(128)S(6)} %copy.10.count.live_count, s32[26,48,128]{2,1,0:T(8,128)} %bitcast.6, bf16[48,65536]{1,0:T(8,128)(2,1)} %table_hbm.1, bf16[48,1024]{1,0:T(8,128)(2,1)} %w_self.1, ...), custom_call_target="tpu_custom_call" | custom-call | flops 60000002048 | bytes 150000000 | tf_op jit(solution)/shard_map/pallas_call | solution.py:174
  54.4 49.0 %shard_map.95.x = bf16[16,2,48,256]{3,2,1,0:T(8,128)(2,1)} custom-call(s32[16,1,128]{2,1,0:T(1,128)} %get-tuple-element.14.counts, s32[26,48,128]{2,1,0:T(8,128)} %bitcast.7, f32[65536,128]{1,0:T(8,128)S(1)} %get-tuple-element.15.nodes), custom_call_target="tpu_custom_call" | custom-call | flops 60000002048 | bytes 150000000 | tf_op jit(solution)/shard_map/pallas_call | solution.py:267
  103.4 46.7 %shard_map.96 = (bf16[384,1024]{1,0:T(8,128)(2,1)}, f32[48,1024]{1,0:T(8,128)}, f32[48,1024]{1,0:T(8,128)}) custom-call(s32[1]{0:T(128)S(6)} %copy.10.count.live_count, bf16[2,768,128]{2,1,0:T(8,128)(2,1)} %get-tuple-element.13.first, bf16[16,2,48,256]{3,2,1,0:T(8,128)(2,1)} %shard_map.95.x, bf16[768,1024]{1,0:T(8,128)(2,1)} %get-tuple-element.16.w_half, ...), custom_call_target="tpu_custom_call" | custom-call | flops 2500000000 | bytes 10000000 | tf_op jit(solution)/shard_map/pallas_call | solution.py:511
  150.1 2.1 %shard_map.97 = (bf16[384,1024]{1,0:T(8,128)(2,1)}, f32[48,1024]{1,0:T(8,128)}, f32[48,1024]{1,0:T(8,128)}) custom-call(bf16[384,1024]{1,0:T(8,128)(2,1)} %get-tuple-element.17.a, f32[48,1024]{1,0:T(8,128)} %get-tuple-element.18.b, f32[48,1024]{1,0:T(8,128)} %get-tuple-element.19.c), custom_call_target="tpu_custom_call" | custom-call | tf_op jit(solution)/shard_map/pallas_call | solution.py:300

commit v6 on v5

--- a/solution.py
+++ b/solution.py
@@ -10,6 +10,7 @@
 BATCH = 8
 CHUNK = 4096
 LOADS = 8
+SHARED = 8
 
 
 def tile_sums(nodes, sums, ids, rows, block, base):
@@ -37,12 +38,16 @@
 
 def first_kernel(
     count, ids_hbm, table_hbm, w_self, w_neigh, nodes, counts, first, weights,
-    table, sums, sent, landed, got, w_got, *rest
+    pair_counts, pair_ids, table, sums, sent, landed, got, w_got, got_pair, ids_pair, *rest
 ):
     fan, _, rows = ids_hbm.shape
     ids = (rest[:fan], rest[fan : 2 * fan])
-    ids_sem, load_sem, c_send, c_recv, x_send, x_recv, w_send, w_recv, w_sem = rest[2 * fan :]
-    core = lax.rem(lax.axis_index("dp"), 2)
+    ids_sem, load_sem, c_send, c_recv, x_send, x_recv, w_send, w_recv, w_sem, i_send, i_recv = rest[
+        2 * fan :
+    ]
+    d = lax.axis_index("dp")
+    core = lax.rem(d, 2)
+    partner = {"dp": d + 1 - 2 * core}
     block, width = table_hbm.shape
     peers = got.shape[0]
     f = lax.axis_index("feat")
@@ -67,6 +72,7 @@
     barrier = pltpu.get_barrier_semaphore()
     for i in range(1, peers):
         pl.semaphore_signal(barrier, inc=1, device_id={"feat": peer(i)}, device_id_type=MESH)
+    pl.semaphore_signal(barrier, inc=1, device_id=partner, device_id_type=MESH)
     got[f] = jnp.zeros(got.shape[1:], jnp.int32) + count[0]
 
     def fill(i, carry):
@@ -83,7 +89,7 @@
         return carry
 
     lax.fori_loop(0, 2, fill, 0)
-    pl.semaphore_wait(barrier, peers - 1)
+    pl.semaphore_wait(barrier, peers)
 
     def count_copy(i):
         return pltpu.make_async_remote_copy(
@@ -118,7 +124,22 @@
                 weight_copy(source, i).start()
             keep.wait()
 
+    def ids_copy(c):
+        return pltpu.make_async_remote_copy(
+            src_ref=ids_hbm.at[:, 3 * (peers - SHARED + c) + 1], dst_ref=ids_pair.at[:, c],
+            send_sem=i_send.at[c], recv_sem=i_recv.at[c], device_id=partner, device_id_type=MESH,
+        )
+
+    for c in range(SHARED):
+        ids_copy(c).start()
     lax.fori_loop(2, LOADS, fill, 0)
+    for i in range(1, peers):
+        count_copy(i).wait()
+    pair_copy = pltpu.make_async_remote_copy(
+        src_ref=got, dst_ref=got_pair, send_sem=i_send.at[SHARED], recv_sem=i_recv.at[SHARED],
+        device_id=partner, device_id_type=MESH,
+    )
+    pair_copy.start()
 
     def pair(p, carry):
         for slot in range(2):
@@ -150,7 +171,6 @@
         landed[part, my_rows] = sent[f, part]
 
     def settle(i, carry):
-        count_copy(i).wait()
         tile_copy(i).wait()
         weight_copy(w_self, i).wait()
         return carry
@@ -159,7 +179,12 @@
     keep = pltpu.make_async_copy(w_got, weights, w_sem)
     keep.start()
     keep.wait()
+    pair_copy.wait()
+    for c in range(SHARED):
+        ids_copy(c).wait()
     counts[...] = got[...]
+    pair_counts[...] = got_pair[...]
+    pair_ids[...] = ids_pair[...]
     first[...] = landed[...]
 
 
@@ -171,15 +196,17 @@
     dma = pltpu.SemaphoreType.DMA
     hbm = pl.BlockSpec(memory_space=pl.ANY)
     vmem = pl.BlockSpec(memory_space=pltpu.VMEM)
-    nodes, counts, first, weights = pl.pallas_call(
+    nodes, *others = pl.pallas_call(
         first_kernel,
         in_specs=[pl.BlockSpec(memory_space=pltpu.SMEM), hbm, hbm, hbm, hbm],
-        out_specs=[vmem, vmem, vmem, hbm],
+        out_specs=[vmem, vmem, vmem, hbm, vmem, vmem],
         out_shape=[
             pltpu.VMEM((width, 128), jnp.float32),
             jax.ShapeDtypeStruct((peers, 1, 128), jnp.int32),
             jax.ShapeDtypeStruct((2, peers * block, rows), jnp.bfloat16),
             jax.ShapeDtypeStruct((peers * block, hidden), w_self.dtype),
+            jax.ShapeDtypeStruct((peers, 1, 128), jnp.int32),
+            jax.ShapeDtypeStruct((fan, SHARED, rows), jnp.int32),
         ],
         scratch_shapes=[
             pltpu.VMEM((block, width), table.dtype),
@@ -188,11 +215,13 @@
             pltpu.VMEM((2, peers * block, rows), jnp.bfloat16),
             pltpu.VMEM((peers, 1, 128), jnp.int32),
             pltpu.VMEM((peers * block, hidden), w_self.dtype),
+            pltpu.VMEM((peers, 1, 128), jnp.int32),
+            pltpu.VMEM((fan, SHARED, rows), jnp.int32),
         ]
         + [pltpu.SMEM((rows,), jnp.int32)] * (2 * fan)
         + [dma((2, fan)), dma((LOADS,))]
         + [dma((peers,))] * 6
-        + [dma],
+        + [dma, dma((SHARED + 1,)), dma((SHARED + 1,))],
         compiler_params=pltpu.CompilerParams(
             collective_id=1, has_side_effects=True, vmem_limit_bytes=28 << 20
         ),
@@ -200,13 +229,14 @@
             flops=60_000_000_000, bytes_accessed=150_000_000, transcendentals=0
         ),
     )(count, ids, table, w_self, w_neigh)
-    return pltpu.with_memory_space_constraint(nodes, pltpu.VMEM), counts, first, weights
-
-
-def gather_kernel(counts, ids_hbm, nodes, out, sums, *rest):
+    return pltpu.with_memory_space_constraint(nodes, pltpu.VMEM), *others
+
+
+def gather_kernel(counts, pair_counts, ids_hbm, pair_ids, nodes, out, helped, sums, given, *rest):
     fan, tiles, rows = ids_hbm.shape
     ids, sem = (rest[:fan], rest[fan : 2 * fan]), rest[2 * fan]
     block = out.shape[2]
+    peers = tiles // 3
     flat = [[ref.reshape(BATCH * rows) for ref in refs] for refs in ids]
 
     def fetch(batch, slot, k):
@@ -216,12 +246,29 @@
 
     for k in range(fan):
         fetch(0, 0, k).start()
+
+    def pair_fetch(k):
+        return pltpu.make_async_copy(pair_ids.at[k], ids[0][k], sem.at[0, k])
+
+    def load_of(ref):
+        return sum((ref[m, 0, 0] - 1 for m in range(peers)), jnp.int32(0))
+
+    more = load_of(counts) - load_of(pair_counts)
+    for side, (ref, surplus) in enumerate(((counts, more), (pair_counts, -more))):
+        limit = lax.div(jnp.maximum(surplus, 0), 2)
+        seen = jnp.int32(0)
+        for c in range(SHARED):
+            second = jnp.where(ref[peers - SHARED + c, 0, 0] >= 2, 1, 0)
+            given[side * SHARED + c] = jnp.where(seen < limit, second, 0)
+            seen = seen + second
 
     def one_batch(batch, slot):
         def tile(j, carry):
             t = batch * BATCH + j
             m, place = lax.div(t, 3), lax.rem(t, 3)
-            live = place < counts[m, 0, 0]
+            away = given[jnp.maximum(m - (peers - SHARED), 0)]
+            away = (away > 0) & (place == 1) & (m >= peers - SHARED)
+            live = (place < counts[m, 0, 0]) & jnp.logical_not(away)
             at = pl.ds(pl.multiple_of(jnp.maximum(place - 1, 0) * rows, rows), rows)
 
             @pl.when(live & (place > 0))
@@ -255,28 +302,60 @@
                     for k in range(fan):
                         fetch(batch + 1, 0, k).start()
 
+                @pl.when(batch == batches - 1)
+                def _():
+                    for k in range(fan):
+                        pair_fetch(k).start()
+
             one_batch(batch, slot)
         return carry
 
     lax.fori_loop(0, batches // 2, pair, 0)
-
-
-def gather(counts, ids, nodes, block):
+    for k in range(fan):
+        pair_fetch(k).wait()
+
+    def help_with(c, carry):
+        taken = given[SHARED + c] > 0
+
+        @pl.when(taken)
+        def _():
+            turned = tile_sums(nodes, sums, flat[0], rows, block, c * rows)
+            helped[c, 0] = turned[:block]
+            helped[c, 1] = turned[block : 2 * block]
+
+        @pl.when(jnp.logical_not(taken))
+        def _():
+            helped[c] = jnp.zeros((2, block, rows), out.dtype)
+
+        return carry
+
+    lax.fori_loop(0, SHARED, help_with, 0)
+
+
+def gather(counts, pair_counts, ids, pair_ids, nodes, block):
     fan, tiles, rows = ids.shape
     vmem = pl.BlockSpec(memory_space=pltpu.VMEM)
     return pl.pallas_call(
         gather_kernel,
-        in_specs=[pl.BlockSpec(memory_space=pltpu.SMEM), pl.BlockSpec(memory_space=pl.ANY), vmem],
-        out_specs=vmem,
-        scratch_shapes=[pltpu.VMEM((rows, 128), jnp.float32)]
+        in_specs=[pl.BlockSpec(memory_space=pltpu.SMEM)] * 2
+        + [pl.BlockSpec(memory_space=pl.ANY)] * 2
+        + [vmem],
+        out_specs=[vmem, vmem],
+        scratch_shapes=[
+            pltpu.VMEM((rows, 128), jnp.float32),
+            pltpu.SMEM((2 * SHARED,), jnp.int32),
+        ]
         + [pltpu.SMEM((BATCH, rows), jnp.int32)] * (2 * fan)
         + [pltpu.SemaphoreType.DMA((2, fan))],
-        out_shape=jax.ShapeDtypeStruct((tiles // 3, 2, block, 2 * rows), jnp.bfloat16),
+        out_shape=[
+            jax.ShapeDtypeStruct((tiles // 3, 2, block, 2 * rows), jnp.bfloat16),
+            jax.ShapeDtypeStruct((SHARED, 2, block, rows), jnp.bfloat16),
+        ],
         compiler_params=pltpu.CompilerParams(vmem_limit_bytes=28 << 20),
         cost_estimate=pl.CostEstimate(
             flops=60_000_000_000, bytes_accessed=150_000_000, transcendentals=0
         ),
-    )(counts, ids, nodes)
+    )(counts, pair_counts, ids, pair_ids, nodes)
 
 
 def finish_kernel(a, b, c, out_a, out_b, out_c, held_a, held_b, held_c, sem):
@@ -309,9 +388,9 @@
 
 
 def layer_kernel(
-    live_count, first, x, w_half, bias, cot, act, out_self, out_neigh,
-    w, mine, turned, delta, other, pair_in, part_a, in_a, part_b, in_b,
-    y_in, half, half_in, x_send, x_recv, p_send, p_recv, r_send, r_recv, y_send, y_recv, h_send, h_recv, local_sem, w_sem,
+    live_count, first, x, helped, w_half, bias, cot, act, out_self, out_neigh,
+    w, mine, x_late, help_in, turned, delta, other, pair_in, part_a, in_a, part_b, in_b,
+    y_in, half, half_in, x_send, x_recv, p_send, p_recv, r_send, r_recv, y_send, y_recv, h_send, h_recv, local_sem, w_sem, help_sem,
 ):
     f, d = lax.axis_index("feat"), lax.axis_index("dp")
     z, xx = lax.div(f, 4), lax.rem(f, 4)
@@ -341,6 +420,14 @@
     for i in range(1, 4):
         pl.semaphore_signal(barrier, inc=1, device_id=y_peer(i), device_id_type=MESH)
     pl.semaphore_wait(barrier, 19)
+
+    def remote(src, dst, send_sem, recv_sem, peer):
+        copy = pltpu.make_async_remote_copy(
+            src_ref=src, dst_ref=dst, send_sem=send_sem, recv_sem=recv_sem,
+            device_id=peer, device_id_type=MESH,
+        )
+        copy.start()
+        return copy
 
     w_other = pltpu.make_async_remote_copy(
         src_ref=w_half, dst_ref=w.at[w_rows], send_sem=w_sem.at[1], recv_sem=w_sem.at[2],
@@ -352,20 +439,49 @@
     early.start()
     my_rows = pl.ds(pl.multiple_of(f * block, block), block)
     later = pl.ds(tile_rows, rows - tile_rows)
-    own = pltpu.make_async_copy(x.at[f], mine.at[:, my_rows, later], local_sem.at[1])
-    own.start()
-    sends = []
-    for i, j in others:
-        copy = pltpu.make_async_remote_copy(
-            src_ref=x.at[feat_peer(i, j)],
+    early_peers = x.shape[0] - SHARED
+    help_copy = remote(helped, help_in, help_sem.at[0], help_sem.at[1], partner)
+    hold = pltpu.make_async_copy(x.at[pl.ds(early_peers, SHARED)], x_late, help_sem.at[2])
+    hold.start()
+
+    def own_copy(source):
+        return pltpu.make_async_copy(source, mine.at[:, my_rows, later], local_sem.at[1])
+
+    def send_copy(i, j, source):
+        return pltpu.make_async_remote_copy(
+            src_ref=source,
             dst_ref=mine.at[:, my_rows, later],
             send_sem=x_send.at[i * 4 + j],
             recv_sem=x_recv.at[i * 4 + j],
             device_id={"feat": feat_peer(i, j)},
             device_id_type=MESH,
         )
-        copy.start()
-        sends.append(copy)
+
+    @pl.when(f < early_peers)
+    def _():
+        own_copy(x.at[f]).start()
+
+    for i, j in others:
+        peer = feat_peer(i, j)
+
+        @pl.when(peer < early_peers)
+        def _():
+            send_copy(i, j, x.at[peer]).start()
+
+    hold.wait()
+    help_copy.wait()
+    x_late[:, :, :, :tile_rows] = x_late[:, :, :, :tile_rows] + help_in[...]
+
+    @pl.when(f >= early_peers)
+    def _():
+        own_copy(x_late.at[f - early_peers]).start()
+
+    for i, j in others:
+        peer = feat_peer(i, j)
+
+        @pl.when(peer >= early_peers)
+        def _():
+            send_copy(i, j, x_late.at[peer - early_peers]).start()
 
     def turn(lo, size):
         def step(i, carry):
@@ -398,9 +514,9 @@
     w_own.wait()
     w_other.wait()
     forward(0, tile_rows)
-    own.wait()
-    for copy in sends:
-        copy.wait()
+    own_copy(x.at[f]).wait()
+    for i, j in others:
+        send_copy(i, j, x.at[feat_peer(i, j)]).wait()
     turn(tile_rows, rows - tile_rows)
     forward(tile_rows, rows - tile_rows)
 
@@ -414,14 +530,6 @@
 
     def product(p, at):
         return jnp.dot(mine[p], delta[:, at], preferred_element_type=jnp.float32)
-
-    def remote(src, dst, send_sem, recv_sem, peer):
-        copy = pltpu.make_async_remote_copy(
-            src_ref=src, dst_ref=dst, send_sem=send_sem, recv_sem=recv_sem,
-            device_id=peer, device_id_type=MESH,
-        )
-        copy.start()
-        return copy
 
     def place(h, phase):
         return xx if (h + phase) % 2 == 0 else z
@@ -500,7 +608,7 @@
         copy.wait_send()
 
 
-def layer(count, first, x, w_half, bias, cot):
+def layer(count, first, x, helped, w_half, bias, cot):
     block, rows = x.shape[2], cot.shape[0]
     half_wide, hidden = w_half.shape
     quarter = hidden // 4
@@ -510,7 +618,7 @@
     dma = pltpu.SemaphoreType.DMA
     return pl.pallas_call(
         layer_kernel,
-        in_specs=[pl.BlockSpec(memory_space=pltpu.SMEM), hbm, hbm, hbm, vmem, vmem],
+        in_specs=[pl.BlockSpec(memory_space=pltpu.SMEM), hbm, hbm, hbm, hbm, vmem, vmem],
         out_specs=[vmem, vmem, vmem],
         out_shape=[
             jax.ShapeDtypeStruct((rows, hidden), bf16),
@@ -520,6 +628,8 @@
         scratch_shapes=[
             pltpu.VMEM((2 * half_wide, hidden), bf16),
             pltpu.VMEM((2, half_wide, rows), bf16),
+            pltpu.VMEM((SHARED, 2, block, 2 * rows // 3), bf16),
+            pltpu.VMEM((SHARED, 2, block, rows // 3), bf16),
             pltpu.VMEM((rows, 2 * half_wide), bf16),
             pltpu.VMEM((rows, hidden), bf16),
             pltpu.VMEM((4, half_wide, quarter), bf16),
@@ -532,7 +642,7 @@
             pltpu.VMEM((2, 2, block, quarter), f32),
             pltpu.VMEM((2, 2, block, quarter), f32),
             dma((16,)), dma((16,)), dma((4,)), dma((4,)), dma((2, 2, 6)), dma((2, 2, 6)),
-            dma((2, 4)), dma((2, 4)), dma((2,)), dma((2,)), dma((2,)), dma((3,)),
+            dma((2, 4)), dma((2, 4)), dma((2,)), dma((2,)), dma((2,)), dma((3,)), dma((3,)),
         ],
         compiler_params=pltpu.CompilerParams(
             collective_id=0, has_side_effects=True, vmem_limit_bytes=56 << 20
@@ -540,18 +650,21 @@
         cost_estimate=pl.CostEstimate(
             flops=2_500_000_000, bytes_accessed=10_000_000, transcendentals=0
         ),
-    )(count, first, x, w_half, bias, cot)
+    )(count, first, x, helped, w_half, bias, cot)
 
 
 def local(node_table, neighbor_ids, tile_counts, w_self, w_neigh, bias, cotangent):
     owned, rows, hidden = cotangent.shape
     ids = neighbor_ids.transpose(1, 0, 2)
-    nodes, counts, first, w_half = first_tiles(tile_counts, ids, node_table, w_self, w_neigh)
-    x = gather(counts, ids, nodes, node_table.shape[0])
+    nodes, counts, first, w_half, pair_counts, pair_ids = first_tiles(
+        tile_counts, ids, node_table, w_self, w_neigh
+    )
+    x, helped = gather(counts, pair_counts, ids, pair_ids, nodes, node_table.shape[0])
     act, grad_self, grad_neigh = layer(
         tile_counts,
         first,
         x,
+        helped,
         w_half,
         bias.reshape(1, hidden),
         cotangent.reshape(owned * rows, hidden),

time: 153 us -> 162 us (1.059)
  Pallas kernels: 151 us -> 160 us
    pallas_call x1, Pallas kernels: 46.7 us -> 62.9 us  [layer(): pl.pallas_call(layer_kernel, in_specs=[pl.BlockSpec(memory_space=pltpu.SM...]
    pallas_call x1, Pallas kernels: 49 us -> 41.9 us  [gather(): pl.pallas_call(gather_kernel, in_specs=[pl.BlockSpec(memory_space=pltpu.S...]
where the time goes in v6:
time: 162 us
  Pallas kernels  160 us (99%)
    pallas_call x1, Pallas kernels, layer(): pl.pallas_call(layer_kernel, in_specs=[pl.BlockSpec(memory_space=pltpu.SM...  62.9 us
    pallas_call x1, Pallas kernels, first_tiles(): pl.pallas_call(first_kernel, in_specs=[pl.BlockSpec(memory_space=pltpu.SM...  53.3 us
    pallas_call x1, Pallas kernels, gather(): pl.pallas_call(gather_kernel, in_specs=[pl.BlockSpec(memory_space=pltpu.S...  41.9 us

profile of v6, /device:TPU:1, one launch (start us, length us, event | category | flops | bytes accessed | tf_op | source)
XLA Modules:
  0.0 161.6 jit_solution(14223253913269455066)
XLA Ops:
  1.3 53.3 %shard_map.94 = (f32[65536,128]{1,0:T(8,128)S(1)}, s32[16,1,128]{2,1,0:T(1,128)}, bf16[2,768,128]{2,1,0:T(8,128)(2,1)}, bf16[768,1024]{1,0:T(8,128)(2,1)}, s32[16,1,128]{2,1,0:T(1,128)}, /*index=5*/s32[26,8,128]{2,1,0:T(8,128)}) custom-call(s32[1]{0:T(128)S(6)} %copy.10.count.live_count, s32[26,48,128]{2,1,0:T(8,128)} %bitcast.6, ...), custom_call_target="tpu_custom_call" | custom-call | flops 60000002048 | bytes 150000000 | tf_op jit(solution)/shard_map/pallas_call | solution.py:199
  54.6 41.9 %shard_map.95 = (bf16[16,2,48,256]{3,2,1,0:T(8,128)(2,1)}, bf16[8,2,48,128]{3,2,1,0:T(8,128)(2,1)}) custom-call(s32[16,1,128]{2,1,0:T(1,128)} %get-tuple-element.18.counts, s32[16,1,128]{2,1,0:T(1,128)} %get-tuple-element.19.pair_counts, s32[26,48,128]{2,1,0:T(8,128)} %bitcast.7, s32[26,8,128]{2,1,0:T(8,128)} %get-tuple-element.20.pair_ids, ...), custom_call_target="tpu_custom_call" | custom-call | flops 60000002048 | bytes 150000000 | tf_op jit(solution)/shard_map/pallas_call | solution.py:338
  96.5 62.9 %shard_map.96 = (bf16[384,1024]{1,0:T(8,128)(2,1)}, f32[48,1024]{1,0:T(8,128)}, f32[48,1024]{1,0:T(8,128)}) custom-call(s32[1]{0:T(128)S(6)} %copy.10.count.live_count, bf16[2,768,128]{2,1,0:T(8,128)(2,1)} %get-tuple-element.17.first, bf16[16,2,48,256]{3,2,1,0:T(8,128)(2,1)} %get-tuple-element.22.x, bf16[8,2,48,128]{3,2,1,0:T(8,128)(2,1)} %get-tuple-element.23.helped, ...), custom_call_target="tpu_custom_call" | custom-call | flops 2500000000 | bytes 10000000 | tf_op jit(solution)/shard_map/pallas_call | solution.py:619
  159.5 2.1 %shard_map.97 = (bf16[384,1024]{1,0:T(8,128)(2,1)}, f32[48,1024]{1,0:T(8,128)}, f32[48,1024]{1,0:T(8,128)}) custom-call(bf16[384,1024]{1,0:T(8,128)(2,1)} %get-tuple-element.25.a, f32[48,1024]{1,0:T(8,128)} %get-tuple-element.26.b, f32[48,1024]{1,0:T(8,128)} %get-tuple-element.27.c), custom_call_target="tpu_custom_call" | custom-call | tf_op jit(solution)/shard_map/pallas_call | solution.py:379
